TPU v7x, 512 devices: a whole 4x4x16 slice. The times are simulated.
512 devices in a mesh: dom: 128 (over z, y, core), feat: 4 (over x).
Axes of the slice: x: 4, y: 4, z: 16, core: 2. Of those that a mesh axis runs over, the one named last changes fastest.
Arguments:
- features: bfloat16 [131072, 256], P('dom', 'feat'), may hold values from -6 to 6
- keep_cols: int32 [128], P('feat'), may hold values from 0 to 63, as said below
- send_rows: int32 [128, 128, 128], P('dom'), may hold values from 0 to 1024, as said below
- tile_cols: int32 [4096], P('dom'), may hold values from 0 to 135
- tile_vals: bfloat16 [4096, 128, 128], P('dom'), may hold values from -0.25 to 0.25
- weight: bfloat16 [128, 256], P('feat'), may hold values from -0.5 to 0.5
- bias: float32 [256], P('feat'), may hold values from -3 to 3
- grad_out: bfloat16 [131072, 256], P('dom', 'feat'), may hold values from -0.015625 to 0.015625
Outputs:
- out: bfloat16 [131072, 256], P('dom', 'feat')
- grad_weight: float32 [128, 256], P(None, 'feat')
- grad_bias: float32 [256], P('feat')
Inputs may be any that keep to these rules, and one draw needn't show every extreme that they name: `keep_cols`: each block of 128 / 4 entries is increasing, holds distinct values and includes 0 and 256 / 4 - 1. send_rows[p, q] lists rows of partition p that partition q reads; the used slots come first and are distinct rows, the rest are 1024; some lists are full and some have one used slot.
All inputs are finite; a program needn't handle non-finite values.
Results may differ from a plain program's by a relative error of at most 0.001.
Values may be sent and summed in bfloat16 or wider, within the bound.
No kernel may reach another device: no remote copies, remote signals or barrier semaphores. Data moves between devices by JAX's collectives and lax.ppermute only.
A program may use at most 64 MiB of HBM per device.

v0:
```python
import jax
import jax.numpy as jnp
from jax import lax
from jax.sharding import PartitionSpec as P


def activation(value):
    return jax.nn.gelu(value, approximate=True)


def shards(features, keep_cols, send_rows, tile_cols, tile_vals, weight, bias, grad_out):
    rows = features.shape[0]
    cols_local = features.shape[1]
    per_block = keep_cols.shape[0]
    block = send_rows.shape[2]
    peers = lax.axis_size("dom")
    select = (jnp.arange(cols_local, dtype=jnp.int32)[:, None] == keep_cols[None, :]).astype(
        jnp.bfloat16
    )
    kept = jnp.dot(features, select, preferred_element_type=jnp.float32).astype(jnp.bfloat16)
    padded = jnp.concatenate([kept, jnp.zeros((1, per_block), jnp.bfloat16)], axis=0)
    outgoing = jnp.take(padded, send_rows[0], axis=0)
    outgoing = outgoing.reshape(peers, block * per_block // 128, 128)
    incoming = lax.all_to_all(outgoing, "dom", split_axis=0, concat_axis=0, tiled=True)
    incoming = incoming.reshape(peers * block, per_block)
    extended = jnp.concatenate([kept, incoming], axis=0).reshape(-1, block, per_block)
    picked = jnp.take(extended, tile_cols, axis=0)
    product = jnp.einsum("tij,tjc->tic", tile_vals, picked, preferred_element_type=jnp.float32)
    row_tiles = rows // block
    tiles_row = tile_cols.shape[0] // row_tiles
    aggregated = (
        product.reshape(row_tiles, tiles_row, block, per_block).sum(axis=1).reshape(rows, per_block)
    )
    aggregated_all = lax.all_gather(aggregated, "feat", axis=1, tiled=True)
    hid_local = bias.shape[0]
    weight_all = lax.all_gather(weight, "feat", axis=0, tiled=True)
    columns = lax.dynamic_slice_in_dim(weight_all, lax.axis_index("feat") * hid_local, hid_local, 1)
    pre = jnp.dot(aggregated_all, columns.astype(jnp.float32), precision=lax.Precision.HIGHEST)
    pre = pre + bias
    out, pull = jax.vjp(activation, pre)
    (grad_pre,) = pull(grad_out.astype(jnp.float32))
    local_weight = jnp.dot(aggregated_all.T, grad_pre, precision=lax.Precision.HIGHEST)
    local_bias = jnp.sum(grad_pre, axis=0)
    grad_weight, grad_bias = lax.psum((local_weight, local_bias), "dom")
    return (out.astype(jnp.bfloat16), grad_weight, grad_bias)


def solution(mesh):
    placed = (
        P("dom", "feat"),
        P("feat"),
        P("dom", None, None),
        P("dom"),
        P("dom", None, None),
        P("feat", None),
        P("feat"),
        P("dom", "feat"),
    )
    return jax.shard_map(
        shards,
        mesh=mesh,
        in_specs=placed,
        out_specs=(P("dom", "feat"), P(None, "feat"), P("feat")),
        check_vma=False,
    )
```

profile of v0, /device:TPU:1, one launch (start us, length us, event | category | flops | bytes accessed | tf_op | source)
XLA Modules:
  0.0 653.0 jit_solution(12834325789895950989)
XLA Ops:
  0.6 0.0 copy-start
  0.6 0.9 fusion.17
  1.6 0.9 compare_and_fusion
  2.5 1.1 fusion
  3.6 0.2 copy.38
  3.8 0.1 concatenate.6.clone
  3.8 57.4 %gather_fusion = bf16[16384,32]{1,0:T(8,128)(2,1)} fusion(bf16[1025,32]{1,0:T(8,128)(2,1)S(1)} %concatenate.6.clone, s32[16384]{0:T(1024)S(1)} %fusion.17), kind=kCustom, calls=%fused_computation | custom fusion | bytes 2162688 | tf_op jit(solution)/shard_map/jit(_take)/gather | solution.py:22
  61.2 5.5 copy.33
  66.8 0.1 copy.31
  66.9 0.1 broadcast_select_fusion
  67.0 0.0 copy-start.2
  67.1 1.7 copy.34
  68.8 20.6 %all-to-all-start = ((bf16[128,32,128]{2,1,0:T(8,128)(2,1)}), bf16[128,32,128]{2,1,0:T(8,128)(2,1)S(1)}, u32[]{:S(2)}, u32[]{:S(2)}) async-start(bf16[128,32,128]{2,1,0:T(8,128)(2,1)} %copy.34), calls=%async_computation | async-start | bytes 2097152 | tf_op jit(solution)/shard_map/all_to_all | solution.py:24
  89.4 10.8 %all_gather.7 = bf16[128,256]{1,0:T(8,128)(2,1)} all-gather(bf16[32,256]{1,0:T(8,128)(2,1)S(1)} %copy-done.2), channel_id=1, replica_groups=mesh['dom'=128,'feat'=4] {'feat'}, dimensions={0}, use_global_device_ids=true | all-gather | bytes 81920 | tf_op jit(solution)/shard_map/all_gather | solution.py:36
  100.2 41.0 %all-to-all-done = bf16[128,32,128]{2,1,0:T(8,128)(2,1)S(1)} async-done(((bf16[128,32,128]{2,1,0:T(8,128)(2,1)}), bf16[128,32,128]{2,1,0:T(8,128)(2,1)S(1)}, u32[]{:S(2)}, u32[]{:S(2)}) %all-to-all-start) | async-done | bytes 1048608 | tf_op jit(solution)/shard_map/all_to_all | solution.py:24
  141.2 3.2 reshape.64
  144.4 3.5 copy.35
  147.9 0.2 copy_bitcast_fusion
  148.2 0.6 gather_fusion.1
  148.8 0.7 bitcast_reduce_fusion
  149.5 10.4 %all_gather.6 = f32[1024,128]{0,1:T(8,128)S(1)} all-gather(f32[1024,32]{0,1:T(8,128)S(1)} %copy_bitcast_fusion.1), channel_id=1, replica_groups=mesh['dom'=128,'feat'=4] {'feat'}, dimensions={1}, use_global_device_ids=true | all-gather | bytes 655360 | tf_op jit(solution)/shard_map/all_gather | solution.py:34
  159.9 1.3 fusion.22
  161.3 0.7 fusion.24
  162.0 491.0 %all-reduce.1 = (f32[128,64]{0,1:T(8,128)}, f32[64]{0:T(128)}) all-reduce(f32[128,64]{0,1:T(8,128)S(1)} %fusion.24, f32[64]{0:T(128)S(1)} %get-tuple-element.5), channel_id=1, replica_groups=mesh['dom'=128,'feat'=4] {'dom'}, use_global_device_ids=true, to_apply=%region_1.2 | all-reduce | flops 8256 | bytes 66048 | tf_op jit(solution)/shard_map/psum | solution.py:44
  (14 shorter events, 0.1 us)
Async XLA Ops:
  0.6 148.1 %copy-start = (bf16[32,128,128]{2,1,0:T(8,128)(2,1)S(1)}, bf16[32,128,128]{2,1,0:T(8,128)(2,1)}, u32[]{:S(2)}) copy-start(bf16[32,128,128]{2,1,0:T(8,128)(2,1)} %param.12) | copy-start | bytes 3145732
  67.0 22.3 %copy-start.2 = (bf16[32,256]{1,0:T(8,128)(2,1)S(1)}, bf16[32,256]{1,0:T(8,128)(2,1)}, u32[]{:S(2)}) copy-start(bf16[32,256]{1,0:T(8,128)(2,1)} %param.13) | copy-start | bytes 49156
  67.0 33.1 %copy-start.4 = (s32[32]{0:T(128)S(1)}, s32[32]{0:T(128)}, u32[]{:S(2)}) copy-start(s32[32]{0:T(128)} %param.11) | copy-start | bytes 388
  68.8 72.4 %all-to-all-start = ((bf16[128,32,128]{2,1,0:T(8,128)(2,1)}), bf16[128,32,128]{2,1,0:T(8,128)(2,1)S(1)}, u32[]{:S(2)}, u32[]{:S(2)}) async-start(bf16[128,32,128]{2,1,0:T(8,128)(2,1)} %copy.34), calls=%async_computation | async-start | bytes 2097152 | tf_op jit(solution)/shard_map/all_to_all | solution.py:24
  148.1 11.8 %copy-start.1 = (bf16[128,256]{1,0:T(8,128)(2,1)S(1)}, bf16[128,256]{1,0:T(8,128)(2,1)}, u32[]{:S(2)}) copy-start(bf16[128,256]{1,0:T(8,128)(2,1)} %all_gather.7) | copy-start | bytes 196612
  148.1 11.8 %copy-start.3 = (bf16[1024,64]{0,1:T(8,128)(2,1)S(1)}, bf16[1024,64]{0,1:T(8,128)(2,1)}, u32[]{:S(2)}) copy-start(bf16[1024,64]{0,1:T(8,128)(2,1)} %param.15) | copy-start | bytes 393220
  148.2 11.8 %copy-start.5 = (f32[64]{0:T(128)S(1)}, f32[64]{0:T(128)}, u32[]{:S(2)}) copy-start(f32[64]{0:T(128)} %param.14) | copy-start | bytes 772
where the time goes:
time: 657 us; the launch traced here: 653 us
  blocking collectives  512 us (78%)
  local copies, waits for them, and re-layouts  72.4 us (11%)
  waiting for transfers between devices  41 us (6%)
  starting transfers between devices  20.6 us (3%)
    psum x1, blocking collectives, shards(): grad_weight, grad_bias = lax.psum((local_weight, local_bias), 'dom')  491 us
    gather x2, local copies, waits for them, and re-layouts, shards(): outgoing = jnp.take(padded, send_rows[0], axis=0)  62.9 us
    all_to_all x1, waiting for transfers between devices, shards(): lax.all_to_all(outgoing, 'dom', split_axis=0, concat_axis=0, tiled=True)  41 us
    all_to_all x1, starting transfers between devices, shards(): lax.all_to_all(outgoing, 'dom', split_axis=0, concat_axis=0, tiled=True)  20.6 us
  transfers between devices with their start and end apart: 1, of which 1 were waited for; matrix products, arithmetic and copies ran while one was open for 0% of the time, Pallas kernels for 0%

commit v1 on v0

v1 whole, which is shorter than its diff:
```python
import functools
import math

import jax
import jax.numpy as jnp
from jax import lax
from jax.experimental import pallas as pl
from jax.experimental.pallas import tpu as pltpu
from jax.sharding import Mesh, PartitionSpec as P

DOM = ("z", "y", "core")
PLANE = ("y", "core")
NT = (((1,), (1,)), ((), ()))
LOW = 256
F32 = jnp.float32
BF16 = jnp.bfloat16


def pick_kernel(keep_ref, features_ref, lists_ref, out_ref, kept_ref, table):
    kept = kept_ref.shape[1]
    block = kept_ref.shape[2]
    highs = features_ref.shape[0] // LOW

    @pl.when(pl.program_id(0) == 0)
    def _():
        lane = lax.broadcasted_iota(jnp.int32, (kept, features_ref.shape[1]), 1)
        select = jnp.where(lane == keep_ref[...], 1.0, 0.0).astype(BF16)
        columns = lax.dot_general(select, features_ref[...], NT, preferred_element_type=F32)
        columns = columns.astype(BF16)
        for tile in range(kept_ref.shape[0]):
            kept_ref[tile] = columns[:, tile * block : (tile + 1) * block]
        for high in range(highs):
            table[high * kept : (high + 1) * kept, :] = columns[:, high * LOW : (high + 1) * LOW]

    for pair in range(lists_ref.shape[0] // 2):
        rows = jnp.concatenate(
            [lists_ref[2 * pair : 2 * pair + 1, :], lists_ref[2 * pair + 1 : 2 * pair + 2, :]], axis=1
        )
        low = rows & (LOW - 1)
        high = rows // LOW
        sub = lax.broadcasted_iota(jnp.int32, (LOW, 2 * block), 0)
        onehot = jnp.where(sub == low, 1.0, 0.0).astype(BF16)
        found = jnp.dot(table[...], onehot, preferred_element_type=F32)
        total = jnp.zeros((kept, 2 * block), F32)
        for step in range(highs):
            total = jnp.where(high == step, found[step * kept : (step + 1) * kept], total)
        total = total.astype(BF16)
        out_ref[2 * pair] = total[:, :block]
        out_ref[2 * pair + 1] = total[:, block:]


def pick(keep_cols, features, lists):
    peers, block = lists.shape
    rows = features.shape[0]
    kept = keep_cols.shape[0]
    step = 16
    return pl.pallas_call(
        pick_kernel,
        grid=(peers // step,),
        in_specs=[
            pl.BlockSpec((kept, 1), lambda i: (0, 0)),
            pl.BlockSpec(features.shape, lambda i: (0, 0)),
            pl.BlockSpec((step, block), lambda i: (i, 0)),
        ],
        out_specs=[
            pl.BlockSpec((step, kept, block), lambda i: (i, 0, 0)),
            pl.BlockSpec((rows // block, kept, block), lambda i: (0, 0, 0)),
        ],
        out_shape=[
            jax.ShapeDtypeStruct((peers, kept, block), BF16),
            jax.ShapeDtypeStruct((rows // block, kept, block), BF16),
        ],
        scratch_shapes=[pltpu.VMEM((rows // LOW * kept, LOW), BF16)],
        compiler_params=pltpu.CompilerParams(vmem_limit_bytes=24 << 20),
        name="pick_rows",
    )(keep_cols[:, None], features, lists)


def aggregate_kernel(tiles_row, cols_ref, own_ref, incoming_ref, vals_ref, out_ref):
    own = own_ref.shape[0]
    block = own_ref.shape[2]
    for tile in range(vals_ref.shape[0] // tiles_row):
        values, picked = [], []
        for term in range(tiles_row):
            at = tile * tiles_row + term
            column = cols_ref[at]
            mine = own_ref[jnp.minimum(column, own - 1)]
            theirs = incoming_ref[jnp.maximum(column - own, 0)]
            picked.append(jnp.where(column < own, mine, theirs))
            values.append(vals_ref[at])
        out_ref[:, tile * block : (tile + 1) * block] = lax.dot_general(
            jnp.concatenate(picked, axis=1), jnp.concatenate(values, axis=1), NT, preferred_element_type=F32
        )


def aggregate(tile_cols, own, incoming, tile_vals):
    tiles, kept, block = own.shape
    vmem = pl.BlockSpec(memory_space=pltpu.VMEM)
    return pl.pallas_call(
        functools.partial(aggregate_kernel, tile_cols.shape[0] // tiles),
        in_specs=[pl.BlockSpec(memory_space=pltpu.SMEM), vmem, vmem, vmem],
        out_specs=vmem,
        out_shape=jax.ShapeDtypeStruct((kept, tiles * block), F32),
        compiler_params=pltpu.CompilerParams(vmem_limit_bytes=24 << 20),
        name="aggregate_tiles",
    )(tile_cols, own, incoming, tile_vals)


def layer_kernel(agg_ref, weight_ref, bias_ref, grad_ref, out_ref, terms_ref):
    hidden, nodes = grad_ref.shape
    step = 256
    depth = agg_ref.shape[0]
    slope = math.sqrt(2.0 / math.pi)
    weight = jnp.concatenate([weight_ref[...]] * 3, axis=1)
    grad_weight = jnp.zeros((hidden, depth), F32)
    grad_bias = jnp.zeros((hidden, 1), F32)
    for start in range(0, nodes, step):
        exact = agg_ref[:, start : start + step]
        first = exact.astype(BF16)
        rest = exact - first.astype(F32)
        second = rest.astype(BF16)
        third = (rest - second.astype(F32)).astype(BF16)
        pre = jnp.dot(weight, jnp.concatenate([first, second, third], axis=0), preferred_element_type=F32)
        pre = pre + bias_ref[...]
        square = pre * pre
        bend = jnp.tanh(slope * (pre + 0.044715 * (pre * square)))
        half = 0.5 * (1.0 + bend)
        out_ref[start : start + step, :] = (pre * half).T.astype(BF16)
        inner = slope * (1.0 + 3 * 0.044715 * square)
        pull = half + 0.5 * pre * ((1.0 - bend) * (1.0 + bend)) * inner
        grad_pre = grad_ref[:, start : start + step].astype(F32) * pull
        grad_bias += jnp.sum(grad_pre, axis=1, keepdims=True)
        upper = grad_pre.astype(BF16)
        lower = (grad_pre - upper.astype(F32)).astype(BF16)
        both = lax.dot_general(
            jnp.concatenate([upper, lower], axis=0),
            jnp.concatenate([first, second], axis=0),
            NT,
            preferred_element_type=F32,
        )
        grad_weight += (both[:hidden, depth:] + both[hidden:, :depth]) + both[:hidden, :depth]
    groups = terms_ref.shape[0]
    terms_ref[:, : hidden // groups, :] = grad_weight.reshape(groups, hidden // groups, depth)
    terms_ref[:, hidden // groups :, :] = jnp.broadcast_to(grad_bias, (hidden, depth)).reshape(
        groups, hidden // groups, depth
    )


def layer(aggregated, weight, bias, grad_out, groups):
    depth, nodes = aggregated.shape
    hidden = weight.shape[0]
    vmem = pl.BlockSpec(memory_space=pltpu.VMEM)
    return pl.pallas_call(
        layer_kernel,
        in_specs=[vmem] * 4,
        out_specs=[vmem] * 2,
        out_shape=[
            jax.ShapeDtypeStruct((nodes, hidden), BF16),
            jax.ShapeDtypeStruct((groups, 2 * hidden // groups, depth), F32),
        ],
        compiler_params=pltpu.CompilerParams(vmem_limit_bytes=24 << 20),
        name="layer_and_gradient",
    )(aggregated, weight, bias[:, None], grad_out)


def spread(array, axis):
    size = lax.axis_size(axis)
    return lax.all_to_all(jnp.broadcast_to(array[None], (size,) + array.shape), axis, 0, 0)


def shards(features, keep_cols, send_rows, tile_cols, tile_vals, weight, bias, grad_out):
    feat = lax.axis_size("feat")
    hidden = bias.shape[0]
    kept = keep_cols.shape[0]
    outgoing, own = pick(keep_cols, features, send_rows[0])
    incoming = lax.all_to_all(outgoing, DOM, 0, 0, tiled=True)
    blocks = weight.reshape(kept, feat, hidden).transpose(1, 2, 0)
    blocks = lax.all_to_all(blocks, "feat", 0, 0)
    columns = blocks.transpose(1, 0, 2).reshape(hidden, feat * kept)
    aggregated = aggregate(tile_cols, own, incoming, tile_vals)
    aggregated = spread(aggregated, "feat").reshape(feat * kept, -1)
    groups = lax.axis_size(PLANE)
    out, terms = layer(aggregated, columns, bias, grad_out.T, groups)
    terms = lax.all_to_all(terms, PLANE, 0, 0).sum(axis=0)
    terms = spread(terms, "z").sum(axis=0)
    terms = spread(terms, PLANE)
    rows = hidden // groups
    grad_weight = terms[:, :rows].reshape(hidden, feat * kept).T
    grad_bias = terms[:, rows:, 0].reshape(hidden)
    return out, grad_weight, grad_bias


def solution(mesh):
    devices = mesh.devices.reshape(16, 4, 2, mesh.shape["feat"])
    fine = Mesh(devices, DOM + ("feat",))
    placed = (
        P(DOM, "feat"),
        P("feat"),
        P(DOM, None, None),
        P(DOM),
        P(DOM, None, None),
        P("feat", None),
        P("feat"),
        P(DOM, "feat"),
    )
    return jax.shard_map(
        shards,
        mesh=fine,
        in_specs=placed,
        out_specs=(P(DOM, "feat"), P(None, "feat"), P("feat")),
        check_vma=False,
    )
```

time: 657 us -> 144 us (0.22)
  blocking collectives: 512 us -> 30.3 us
  local copies, waits for them, and re-layouts: 72.4 us -> 7.18 us
  waiting for transfers between devices: 41 us -> 64.3 us
  starting transfers between devices: 20.6 us -> 35.3 us
    psum x1 -> x0, blocking collectives: 491 us -> none  [shards(): grad_weight, grad_bias = lax.psum((local_weight, local_bias), 'dom')]
    gather x3 -> x0, local copies, waits for them, and re-layouts: 63.5 us -> none  [the longest x2 62.9 us: shards(): outgoing = jnp.take(padded, send_rows[0], axis=0)]
    all_to_all x0 -> x2, blocking collectives: none -> 30.3 us  [the longest x1 15.5 us: shards(): terms = lax.all_to_all(terms, PLANE, 0, 0).sum(axis=0)]
    all_to_all x1 -> x4, waiting for transfers between devices: 41 us -> 64.3 us  [the longest x1 51 us: shards(): incoming = lax.all_to_all(outgoing, DOM, 0, 0, tiled=True)]
    all_gather x2 -> x0, blocking collectives: 21.2 us -> none  [the longest x1 10.8 us: shards(): weight_all = lax.all_gather(weight, 'feat', axis=0, tiled=True)]
    all_to_all x1 -> x4, starting transfers between devices: 20.6 us -> 35.3 us  [the longest x1 20.7 us: shards(): incoming = lax.all_to_all(outgoing, DOM, 0, 0, tiled=True)]
  transfers between devices with their start and end apart: 1 -> 4, of which waited for: 1 -> 4; matrix products, arithmetic and copies ran while one was open for 0% -> 1% of each run, Pallas kernels for 0% -> 1%
where the time goes in v1:
time: 144 us
  waiting for transfers between devices  64.3 us (45%)
  starting transfers between devices  35.3 us (25%)
  blocking collectives  30.3 us (21%)
  local copies, waits for them, and re-layouts  7.18 us (5%)
  Pallas kernels  6 us (4%)
    all_to_all x1, waiting for transfers between devices, shards(): incoming = lax.all_to_all(outgoing, DOM, 0, 0, tiled=True)  51 us
    all_to_all x1, starting transfers between devices, shards(): incoming = lax.all_to_all(outgoing, DOM, 0, 0, tiled=True)  20.7 us
    all_to_all x1, blocking collectives, shards(): terms = lax.all_to_all(terms, PLANE, 0, 0).sum(axis=0)  15.5 us
    all_to_all x1, blocking collectives, spread(): lax.all_to_all(jnp.broadcast_to(array[None], (size,) + array.shape), axis...  14.8 us
    all_to_all x2, waiting for transfers between devices, spread(): lax.all_to_all(jnp.broadcast_to(array[None], (size,) + array.shape), axis...  10.7 us
    all_to_all x2, starting transfers between devices, spread(): lax.all_to_all(jnp.broadcast_to(array[None], (size,) + array.shape), axis...  10.6 us
    pallas_call x1, Pallas kernels, pick(): pl.pallas_call(pick_kernel, grid=(peers // step,), in_specs=[pl.BlockSpec...  4.48 us
    all_to_all x1, starting transfers between devices, shards(): blocks = lax.all_to_all(blocks, 'feat', 0, 0)  4.01 us
  transfers between devices with their start and end apart: 4, of which 4 were waited for; matrix products, arithmetic and copies ran while one was open for 1% of the time, Pallas kernels for 1%

profile of v1, /device:TPU:1, one launch (start us, length us, event | category | flops | bytes accessed | tf_op | source)
XLA Modules:
  0.0 143.9 jit_solution(3416060945309211232)
XLA Ops:
  0.6 0.6 copy-done.6
  1.4 1.1 copy.37.features_ref
  2.5 4.5 %pick_rows.1 = (bf16[128,32,128]{2,1,0:T(8,128)(2,1)}, bf16[8,32,128]{2,1,0:T(8,128)(2,1)S(1)}) custom-call(s32[32,1]{1,0:T(8,128)S(1)} %copy.36.keep_ref, bf16[1024,64]{1,0:T(8,128)(2,1)S(1)} %copy.37.features_ref, s32[128,128]{1,0:T(8,128)S(1)} %bitcast.23), custom_call_target="tpu_custom_call" | custom-call | tf_op jit(solution)/shard_map/pick_rows/pallas_call | solution.py:57
  7.0 20.7 %all-to-all-start = ((bf16[128,32,128]{2,1,0:T(8,128)(2,1)}), bf16[128,32,128]{2,1,0:T(8,128)(2,1)S(1)}, u32[]{:S(2)}, u32[]{:S(2)}) async-start(bf16[128,32,128]{2,1,0:T(8,128)(2,1)} %get-tuple-element.8), calls=%async_computation | async-start | bytes 2097152 | tf_op jit(solution)/shard_map/all_to_all | solution.py:176
  27.8 0.7 reshape.26
  28.5 51.0 %all-to-all-done.incoming_ref = bf16[128,32,128]{2,1,0:T(8,128)(2,1)S(1)} async-done(((bf16[128,32,128]{2,1,0:T(8,128)(2,1)}), bf16[128,32,128]{2,1,0:T(8,128)(2,1)S(1)}, u32[]{:S(2)}, u32[]{:S(2)}) %all-to-all-start) | async-done | bytes 1048608 | tf_op jit(solution)/shard_map/all_to_all | solution.py:176
  79.5 4.0 %all-to-all-start.2 = ((bf16[4,2,1024]{2,1,0:T(2,128)(2,1)}), bf16[4,2,1024]{2,1,0:T(2,128)(2,1)S(1)}, u32[]{:S(2)}, u32[]{:S(2)}) async-start(bf16[4,2,1024]{2,1,0:T(2,128)(2,1)} %reshape.26), calls=%async_computation.2 | async-start | bytes 32768 | tf_op jit(solution)/shard_map/all_to_all | solution.py:178
  83.5 0.7 copy-done.3
  84.2 1.0 aggregate_tiles.1
  85.2 2.6 %all-to-all-done.2 = bf16[4,2,1024]{2,1,0:T(2,128)(2,1)S(1)} async-done(((bf16[4,2,1024]{2,1,0:T(2,128)(2,1)}), bf16[4,2,1024]{2,1,0:T(2,128)(2,1)S(1)}, u32[]{:S(2)}, u32[]{:S(2)}) %all-to-all-start.2) | async-done | bytes 16416 | tf_op jit(solution)/shard_map/all_to_all | solution.py:178
  87.8 0.9 broadcast_in_dim.11
  88.6 3.6 %all-to-all-start.1 = ((f32[4,32,1024]{2,1,0:T(8,128)}), f32[4,32,1024]{2,1,0:T(8,128)S(1)}, u32[]{:S(2)}, u32[]{:S(2)}) async-start(f32[4,32,1024]{2,1,0:T(8,128)} %broadcast_in_dim.11), calls=%async_computation.1 | async-start | bytes 1048576 | tf_op jit(solution)/shard_map/all_to_all | solution.py:168
  92.2 0.1 copy.40.bias_ref
  92.3 0.1 reshape.27
  92.5 6.6 %all-to-all-done.1 = f32[4,32,1024]{2,1,0:T(8,128)S(1)} async-done(((f32[4,32,1024]{2,1,0:T(8,128)}), f32[4,32,1024]{2,1,0:T(8,128)S(1)}, u32[]{:S(2)}, u32[]{:S(2)}) %all-to-all-start.1) | async-done | bytes 524320 | tf_op jit(solution)/shard_map/all_to_all | solution.py:168
  99.1 0.5 layer_and_gradient.1
  99.7 15.5 %all_to_all.30 = f32[8,16,128]{2,1,0:T(8,128)S(1)} all-to-all(f32[8,16,128]{2,1,0:T(8,128)S(1)} %get-tuple-element.10), channel_id=1, replica_groups=mesh['z'=16,'y'=4,'core'=2,'feat'=4] {'y','core'}, dimensions={0} | all-to-all | bytes 131072 | tf_op jit(solution)/shard_map/all_to_all | solution.py:184
  115.2 14.8 %all_to_all.31 = f32[16,16,128]{2,1,0:T(8,128)S(1)} all-to-all(f32[16,16,128]{2,1,0:T(8,128)S(1)} %broadcast_in_dim.13), channel_id=1, replica_groups=mesh['z'=16,'y'=4,'core'=2,'feat'=4] {'z'}, dimensions={0} | all-to-all | bytes 262144 | tf_op jit(solution)/shard_map/all_to_all | solution.py:168
  130.1 0.6 broadcast_in_dim.28
  130.7 7.0 %all-to-all-start.5 = ((f32[8,16,128]{2,1,0:T(8,128)}), f32[8,16,128]{2,1,0:T(8,128)S(1)}, u32[]{:S(2)}, u32[]{:S(2)}) async-start(f32[8,16,128]{2,1,0:T(8,128)} %broadcast_in_dim.28), calls=%async_computation.5 | async-start | bytes 131072 | tf_op jit(solution)/shard_map/all_to_all | solution.py:168
  137.7 0.8 copy.41
  138.5 4.1 %all-to-all-done.5 = f32[8,16,128]{2,1,0:T(8,128)S(1)} async-done(((f32[8,16,128]{2,1,0:T(8,128)}), f32[8,16,128]{2,1,0:T(8,128)S(1)}, u32[]{:S(2)}, u32[]{:S(2)}) %all-to-all-start.5) | async-done | bytes 65568 | tf_op jit(solution)/shard_map/all_to_all | solution.py:168
  142.6 0.6 reshape_squeeze.3
  143.2 0.6 slice_bitcast_fusion
  (20 shorter events, 0.4 us)
Async XLA Ops:
  0.6 0.7 copy-start.6
  1.4 1.1 copy-start.2
  7.0 20.7 %copy-start.4 = (bf16[32,256]{1,0:T(8,128)(2,1)S(1)}, bf16[32,256]{1,0:T(8,128)(2,1)}, u32[]{:S(2)}) copy-start(bf16[32,256]{1,0:T(8,128)(2,1)} %param.13) | copy-start | bytes 49156
  7.0 76.6 %copy-start = (bf16[32,128,128]{2,1,0:T(8,128)(2,1)S(1)}, bf16[32,128,128]{2,1,0:T(8,128)(2,1)}, u32[]{:S(2)}) copy-start(bf16[32,128,128]{2,1,0:T(8,128)(2,1)} %vals_ref.1) | copy-start | bytes 3145732
  7.0 72.5 %all-to-all-start = ((bf16[128,32,128]{2,1,0:T(8,128)(2,1)}), bf16[128,32,128]{2,1,0:T(8,128)(2,1)S(1)}, u32[]{:S(2)}, u32[]{:S(2)}) async-start(bf16[128,32,128]{2,1,0:T(8,128)(2,1)} %get-tuple-element.8), calls=%async_computation | async-start | bytes 2097152 | tf_op jit(solution)/shard_map/all_to_all | solution.py:176
  79.5 8.2 %all-to-all-start.2 = ((bf16[4,2,1024]{2,1,0:T(2,128)(2,1)}), bf16[4,2,1024]{2,1,0:T(2,128)(2,1)S(1)}, u32[]{:S(2)}, u32[]{:S(2)}) async-start(bf16[4,2,1024]{2,1,0:T(2,128)(2,1)} %reshape.26), calls=%async_computation.2 | async-start | bytes 32768 | tf_op jit(solution)/shard_map/all_to_all | solution.py:178
  83.5 0.7 copy-start.3
  88.6 3.6 %copy-start.5 = (f32[64]{0:T(128)S(1)}, f32[64]{0:T(128)}, u32[]{:S(2)}) copy-start(f32[64]{0:T(128)} %param.14) | copy-start | bytes 772
  88.6 10.5 %all-to-all-start.1 = ((f32[4,32,1024]{2,1,0:T(8,128)}), f32[4,32,1024]{2,1,0:T(8,128)S(1)}, u32[]{:S(2)}, u32[]{:S(2)}) async-start(f32[4,32,1024]{2,1,0:T(8,128)} %broadcast_in_dim.11), calls=%async_computation.1 | async-start | bytes 1048576 | tf_op jit(solution)/shard_map/all_to_all | solution.py:168
  92.2 6.9 %copy-start.1 = (bf16[1024,64]{0,1:T(8,128)(2,1)S(1)}, bf16[1024,64]{0,1:T(8,128)(2,1)}, u32[]{:S(2)}) copy-start(bf16[1024,64]{0,1:T(8,128)(2,1)} %param.15) | copy-start | bytes 393220
  130.7 11.9 %all-to-all-start.5 = ((f32[8,16,128]{2,1,0:T(8,128)}), f32[8,16,128]{2,1,0:T(8,128)S(1)}, u32[]{:S(2)}, u32[]{:S(2)}) async-start(f32[8,16,128]{2,1,0:T(8,128)} %broadcast_in_dim.28), calls=%async_computation.5 | async-start | bytes 131072 | tf_op jit(solution)/shard_map/all_to_all | solution.py:168

commit v2 on v1

v2 whole, which is shorter than its diff:
```python
import functools
import math

import jax
import jax.numpy as jnp
from jax import lax
from jax.experimental import pallas as pl
from jax.experimental.pallas import tpu as pltpu
from jax.sharding import Mesh, PartitionSpec as P

DOM = ("z_far", "z_near", "y", "core")
NEAR = ("z_near", "y", "core")
PLANE = ("y", "core")
RING = ("z_far", "z_near")
NT = (((1,), (1,)), ((), ()))
LOW = 256
CODE = 128
F32 = jnp.float32
BF16 = jnp.bfloat16


def keep_kernel(keep_ref, features_ref, lists_ref, out_ref):
    planes, rows, block = out_ref.shape
    kept = keep_ref.shape[0]
    nodes = features_ref.shape[1]
    lists = lists_ref.shape[0] // planes
    lane = lax.broadcasted_iota(jnp.int32, (kept, features_ref.shape[0]), 1)
    select = jnp.where(lane == keep_ref[...], 1.0, 0.0).astype(BF16)
    columns = jnp.dot(select, features_ref[...], preferred_element_type=F32).astype(BF16)
    row = lists_ref[...]
    code = lax.shift_left(CODE + (row & (CODE - 1)), row // CODE)
    code = (code.astype(F32) * (1.0 / CODE)).astype(BF16)
    for plane in range(planes):
        for tile in range(nodes // block):
            out_ref[plane, tile * kept : (tile + 1) * kept, :] = columns[:, tile * block : (tile + 1) * block]
        out_ref[plane, rows - lists :, :] = code[plane * lists : (plane + 1) * lists]


def keep(keep_cols, features, lists, planes):
    peers, block = lists.shape
    nodes = features.shape[1]
    kept = keep_cols.shape[0]
    rows = nodes // block * kept + peers // planes
    vmem = pl.BlockSpec(memory_space=pltpu.VMEM)
    return pl.pallas_call(
        keep_kernel,
        in_specs=[vmem] * 3,
        out_specs=vmem,
        out_shape=jax.ShapeDtypeStruct((planes, rows, block), BF16),
        compiler_params=pltpu.CompilerParams(vmem_limit_bytes=24 << 20),
        name="keep_columns",
    )(keep_cols[:, None], features, lists)


def pick_kernel(held_ref, out_ref):
    lists, _, kept, block = out_ref.shape
    tiles = (held_ref.shape[1] - lists) // kept
    span = LOW // block
    highs = tiles // span
    table = jnp.concatenate(
        [
            jnp.concatenate([held_ref[0, t * kept : (t + 1) * kept, :] for t in range(h * span, (h + 1) * span)], axis=1)
            for h in range(highs)
        ],
        axis=0,
    )
    code = (held_ref[0, tiles * kept :, :].astype(F32) * CODE).astype(jnp.int32)
    shift = jnp.zeros((lists, block), jnp.int32)
    for step in range(1, tiles + 1):
        shift += jnp.where(code >= CODE << step, 1, 0)
    row = shift * CODE + (lax.shift_right_logical(code, shift) - CODE)
    sub = lax.broadcasted_iota(jnp.int32, (LOW, 2 * block), 0)
    for pair in range(lists // 2):
        rows = jnp.concatenate([row[2 * pair : 2 * pair + 1, :], row[2 * pair + 1 : 2 * pair + 2, :]], axis=1)
        low = rows & (LOW - 1)
        high = rows // LOW
        onehot = jnp.where(sub == low, 1.0, 0.0).astype(BF16)
        found = jnp.dot(table, onehot, preferred_element_type=F32)
        total = jnp.zeros((kept, 2 * block), F32)
        for step in range(highs):
            total = jnp.where(high == step, found[step * kept : (step + 1) * kept], total)
        total = total.astype(BF16)
        out_ref[2 * pair, 0] = total[:, :block]
        out_ref[2 * pair + 1, 0] = total[:, block:]


def pick(held, lists, kept):
    planes, rows, block = held.shape
    return pl.pallas_call(
        pick_kernel,
        grid=(planes,),
        in_specs=[pl.BlockSpec((1, rows, block), lambda i: (i, 0, 0))],
        out_specs=pl.BlockSpec((lists, 1, kept, block), lambda i: (0, i, 0, 0)),
        out_shape=jax.ShapeDtypeStruct((lists, planes, kept, block), BF16),
        compiler_params=pltpu.CompilerParams(vmem_limit_bytes=24 << 20),
        name="pick_rows",
    )(held)


def aggregate_kernel(tiles_row, cols_ref, own_ref, incoming_ref, vals_ref, out_ref):
    kept, block = incoming_ref.shape[2:]
    own = vals_ref.shape[0] // tiles_row
    near = incoming_ref.shape[0]
    for tile in range(vals_ref.shape[0] // tiles_row):
        values, picked = [], []
        for term in range(tiles_row):
            at = tile * tiles_row + term
            column = cols_ref[at]
            mine = own_ref[pl.ds(pl.multiple_of(jnp.minimum(column, own - 1) * kept, kept), kept), :]
            sender = jnp.maximum(column - own, 0)
            theirs = incoming_ref[sender % near, sender // near]
            picked.append(jnp.where(column < own, mine, theirs))
            values.append(vals_ref[at])
        total = lax.dot_general(
            jnp.concatenate(picked, axis=1), jnp.concatenate(values, axis=1), NT, preferred_element_type=F32
        )
        for copy in range(out_ref.shape[0]):
            out_ref[copy, :, tile * block : (tile + 1) * block] = total


def aggregate(tile_cols, own, incoming, tile_vals, copies):
    kept, block = incoming.shape[2:]
    tiles = own.shape[0] // kept
    vmem = pl.BlockSpec(memory_space=pltpu.VMEM)
    return pl.pallas_call(
        functools.partial(aggregate_kernel, tile_cols.shape[0] // tiles),
        in_specs=[pl.BlockSpec(memory_space=pltpu.SMEM), vmem, vmem, vmem],
        out_specs=vmem,
        out_shape=jax.ShapeDtypeStruct((copies, kept, tiles * block), F32),
        compiler_params=pltpu.CompilerParams(vmem_limit_bytes=24 << 20),
        name="aggregate_tiles",
    )(tile_cols, own, incoming, tile_vals)


def layer_kernel(agg_ref, weight_ref, bias_ref, grad_ref, out_ref, terms_ref):
    hidden, nodes = grad_ref.shape
    step = 256
    depth = agg_ref.shape[0]
    slope = math.sqrt(2.0 / math.pi)
    weight = jnp.concatenate([weight_ref[...]] * 3, axis=1)
    grad_weight = jnp.zeros((hidden, depth), F32)
    grad_bias = jnp.zeros((hidden, 1), F32)
    for start in range(0, nodes, step):
        exact = agg_ref[:, start : start + step]
        first = exact.astype(BF16)
        rest = exact - first.astype(F32)
        second = rest.astype(BF16)
        third = (rest - second.astype(F32)).astype(BF16)
        pre = jnp.dot(weight, jnp.concatenate([first, second, third], axis=0), preferred_element_type=F32)
        pre = pre + bias_ref[...]
        square = pre * pre
        bend = jnp.tanh(slope * (pre + 0.044715 * (pre * square)))
        half = 0.5 * (1.0 + bend)
        out_ref[:, start : start + step] = (pre * half).astype(BF16)
        inner = slope * (1.0 + 3 * 0.044715 * square)
        pull = half + 0.5 * pre * ((1.0 - bend) * (1.0 + bend)) * inner
        grad_pre = grad_ref[:, start : start + step].astype(F32) * pull
        grad_bias += jnp.sum(grad_pre, axis=1, keepdims=True)
        upper = grad_pre.astype(BF16)
        lower = (grad_pre - upper.astype(F32)).astype(BF16)
        both = lax.dot_general(
            jnp.concatenate([upper, lower], axis=0),
            jnp.concatenate([first, second], axis=0),
            NT,
            preferred_element_type=F32,
        )
        grad_weight += (both[:hidden, depth:] + both[hidden:, :depth]) + both[:hidden, :depth]
    groups = terms_ref.shape[0]
    terms_ref[:, : hidden // groups, :] = grad_weight.reshape(groups, hidden // groups, depth)
    terms_ref[:, hidden // groups :, :] = jnp.broadcast_to(grad_bias, (hidden, depth)).reshape(
        groups, hidden // groups, depth
    )


def layer(aggregated, weight, bias, grad_out, groups):
    depth, nodes = aggregated.shape
    hidden = weight.shape[0]
    vmem = pl.BlockSpec(memory_space=pltpu.VMEM)
    return pl.pallas_call(
        layer_kernel,
        in_specs=[vmem] * 4,
        out_specs=[vmem] * 2,
        out_shape=[
            jax.ShapeDtypeStruct((hidden, nodes), BF16),
            jax.ShapeDtypeStruct((groups, 2 * hidden // groups, depth), F32),
        ],
        compiler_params=pltpu.CompilerParams(vmem_limit_bytes=24 << 20),
        name="layer_and_gradient",
    )(aggregated, weight, bias[:, None], grad_out)


def spread(array, axis):
    size = lax.axis_size(axis)
    return lax.all_to_all(jnp.broadcast_to(array[None], (size,) + array.shape), axis, 0, 0)


def shards(features, keep_cols, send_rows, tile_cols, tile_vals, weight, bias, grad_out):
    feat = lax.axis_size("feat")
    hidden = bias.shape[0]
    kept = keep_cols.shape[0]
    planes = lax.axis_size("z_far")
    near = lax.axis_size(NEAR)
    block = send_rows.shape[2]
    outgoing = keep(keep_cols, features.T, send_rows[0], planes)
    own = outgoing[0, : features.shape[0] // block * kept]
    held = lax.all_to_all(outgoing, "z_far", 0, 0)
    picked = pick(held, near, kept).reshape(near, planes * kept, block)
    incoming = lax.all_to_all(picked, NEAR, 0, 0)
    incoming = incoming.reshape(near, planes, kept, block)
    weight_all = lax.all_gather(weight, "feat", axis=0, tiled=True)
    columns = lax.dynamic_slice_in_dim(weight_all, lax.axis_index("feat") * hidden, hidden, 1).T
    incoming, columns = lax.optimization_barrier((incoming, columns))
    aggregated = aggregate(tile_cols, own, incoming, tile_vals, feat)
    aggregated = lax.all_to_all(aggregated, "feat", 0, 0).reshape(feat * kept, -1)
    groups = lax.axis_size(PLANE)
    out, terms = layer(aggregated, columns, bias, grad_out.T, groups)
    terms = lax.all_to_all(terms, PLANE, 0, 0).sum(axis=0)
    terms = spread(terms, RING).sum(axis=0)
    terms = spread(terms, PLANE)
    rows = hidden // groups
    grad_weight = terms[:, :rows].reshape(hidden, feat * kept)
    grad_bias = terms[:, rows:, 0]
    return out.T, grad_weight.T, grad_bias.reshape(hidden)


def solution(mesh):
    devices = mesh.devices.reshape(4, 4, 4, 2, mesh.shape["feat"])
    fine = Mesh(devices, DOM + ("feat",))
    placed = (
        P(DOM, "feat"),
        P("feat"),
        P(DOM, None, None),
        P(DOM),
        P(DOM, None, None),
        P("feat", None),
        P("feat"),
        P(DOM, "feat"),
    )
    return jax.shard_map(
        shards,
        mesh=fine,
        in_specs=placed,
        out_specs=(P(DOM, "feat"), P(None, "feat"), P("feat")),
        check_vma=False,
    )
```

time: 144 us -> 132 us (0.917)
  blocking collectives: 30.3 us -> 74.9 us
  waiting for transfers between devices: 64.3 us -> 24.9 us
  starting transfers between devices: 35.3 us -> 19.3 us
  local copies, waits for them, and re-layouts: 7.18 us -> 5.38 us
    all_to_all x4 -> x2, waiting for transfers between devices: 64.3 us -> 24.9 us  [the longest x1 16.2 us: shards(): incoming = lax.all_to_all(picked, NEAR, 0, 0)]
    all_to_all x0 -> x1, blocking collectives: none -> 30 us  [shards(): held = lax.all_to_all(outgoing, 'z_far', 0, 0)]
    all_to_all x4 -> x2, starting transfers between devices: 35.3 us -> 19.3 us  [the longest x1 15.2 us: shards(): incoming = lax.all_to_all(picked, NEAR, 0, 0)]
    all_to_all x1 -> x2, blocking collectives: 14.8 us -> 25.4 us  [spread(): lax.all_to_all(jnp.broadcast_to(array[None], (size,) + array.shape), axis...]
    all_gather x0 -> x1, blocking collectives: none -> 10.2 us  [shards(): weight_all = lax.all_gather(weight, 'feat', axis=0, tiled=True)]
    all_to_all x1, blocking collectives: 15.5 us -> 9.35 us  [shards(): terms = lax.all_to_all(terms, PLANE, 0, 0).sum(axis=0)]
    broadcast_in_dim x3 -> x2, local copies, waits for them, and re-layouts: 1.5 us -> 0.02 us  [spread(): jnp.broadcast_to(array[None], (size,) + array.shape)]
    pallas_call x1 -> x2, Pallas kernels: 4.48 us -> 3.71 us  [the longest x1 3.5 us: pick(): pl.pallas_call(pick_kernel, grid=(planes,), in_specs=[pl.BlockSpec((1, ro...]
  transfers between devices with their start and end apart: 4 -> 2, of which waited for: 4 -> 2; matrix products, arithmetic and copies ran while one was open for 1% -> 0% of each run, Pallas kernels for 1% -> 0%
where the time goes in v2:
time: 132 us
  blocking collectives  74.9 us (57%)
  waiting for transfers between devices  24.9 us (19%)
  starting transfers between devices  19.3 us (15%)
  Pallas kernels  6.56 us (5%)
  local copies, waits for them, and re-layouts  5.38 us (4%)
    all_to_all x1, blocking collectives, shards(): held = lax.all_to_all(outgoing, 'z_far', 0, 0)  30 us
    all_to_all x2, blocking collectives, spread(): lax.all_to_all(jnp.broadcast_to(array[None], (size,) + array.shape), axis...  25.4 us
    all_to_all x1, waiting for transfers between devices, shards(): incoming = lax.all_to_all(picked, NEAR, 0, 0)  16.2 us
    all_to_all x1, starting transfers between devices, shards(): incoming = lax.all_to_all(picked, NEAR, 0, 0)  15.2 us
    all_gather x1, blocking collectives, shards(): weight_all = lax.all_gather(weight, 'feat', axis=0, tiled=True)  10.2 us
    all_to_all x1, blocking collectives, shards(): terms = lax.all_to_all(terms, PLANE, 0, 0).sum(axis=0)  9.35 us
    all_to_all x1, waiting for transfers between devices, shards(): lax.all_to_all(aggregated, 'feat', 0, 0).reshape(feat * kept, -1)  8.68 us
    all_to_all x1, starting transfers between devices, shards(): lax.all_to_all(aggregated, 'feat', 0, 0).reshape(feat * kept, -1)  4.14 us
  transfers between devices with their start and end apart: 2, of which 2 were waited for; matrix products, arithmetic and copies ran while one was open for 0% of the time, Pallas kernels for 0%

profile of v2, /device:TPU:1, one launch (start us, length us, event | category | flops | bytes accessed | tf_op | source)
XLA Modules:
  0.0 131.8 jit_solution(2982118789966646133)
XLA Ops:
  0.6 0.6 copy-done.7
  1.3 0.1 copy.21.keep_ref
  1.4 0.9 copy-done.1
  2.3 0.8 copy-done.3
  3.1 0.2 keep_columns.1
  3.3 30.0 %all_to_all.30.held_ref = bf16[4,288,128]{2,1,0:T(8,128)(2,1)S(1)} all-to-all(bf16[4,288,128]{2,1,0:T(8,128)(2,1)S(1)} %keep_columns.1), channel_id=1, replica_groups=mesh['z_far'=4,'z_near'=4,'y'=4,'core'=2,'feat'=4] {'z_far'}, dimensions={0} | all-to-all | bytes 589824 | tf_op jit(solution)/shard_map/all_to_all | solution.py:206
  33.3 3.5 %pick_rows.1 = bf16[32,4,32,128]{3,2,1,0:T(8,128)(2,1)} custom-call(bf16[4,288,128]{2,1,0:T(8,128)(2,1)S(1)} %all_to_all.30.held_ref), custom_call_target="tpu_custom_call" | custom-call | tf_op jit(solution)/shard_map/pick_rows/pallas_call | solution.py:89
  36.9 15.2 %all-to-all-start.1 = ((bf16[32,128,128]{2,1,0:T(8,128)(2,1)}), bf16[32,128,128]{2,1,0:T(8,128)(2,1)S(1)}, u32[]{:S(2)}, u32[]{:S(2)}) async-start(bf16[32,128,128]{2,1,0:T(8,128)(2,1)} %bitcast.4), calls=%async_computation.1 | async-start | bytes 2097152 | tf_op jit(solution)/shard_map/all_to_all | solution.py:208
  52.0 10.2 %all_gather.3 = bf16[128,256]{1,0:T(8,128)(2,1)S(1)} all-gather(bf16[32,256]{1,0:T(8,128)(2,1)S(1)} %copy-done.5), channel_id=1, replica_groups=mesh['z_far'=4,'z_near'=4,'y'=4,'core'=2,'feat'=4] {'feat'}, dimensions={0}, use_global_device_ids=true | all-gather | bytes 81920 | tf_op jit(solution)/shard_map/all_gather | solution.py:210
  62.3 0.1 copy.24
  62.4 16.2 %all-to-all-done.1 = bf16[32,128,128]{2,1,0:T(8,128)(2,1)S(1)} async-done(((bf16[32,128,128]{2,1,0:T(8,128)(2,1)}), bf16[32,128,128]{2,1,0:T(8,128)(2,1)S(1)}, u32[]{:S(2)}, u32[]{:S(2)}) %all-to-all-start.1) | async-done | bytes 1048608 | tf_op jit(solution)/shard_map/all_to_all | solution.py:208
  78.6 0.7 copy-done.4
  79.3 1.8 %aggregate_tiles.1 = f32[4,32,1024]{2,1,0:T(8,128)} custom-call(s32[32]{0:T(128)S(1)} %copy-done.4, bf16[256,128]{1,0:T(8,128)(2,1)S(1)} %slice_bitcast_fusion.own_ref, bf16[32,4,32,128]{3,2,1,0:T(8,128)(2,1)S(1)} %bitcast.16, bf16[32,128,128]{2,1,0:T(8,128)(2,1)S(1)} %copy-done), custom_call_target="tpu_custom_call" | custom-call | tf_op jit(solution)/shard_map/aggregate_tiles/pallas_call | solution.py:125
  81.1 4.1 %all-to-all-start.2 = ((f32[4,32,1024]{2,1,0:T(8,128)}), f32[4,32,1024]{2,1,0:T(8,128)S(1)}, u32[]{:S(2)}, u32[]{:S(2)}) async-start(f32[4,32,1024]{2,1,0:T(8,128)} %aggregate_tiles.1), calls=%async_computation.2 | async-start | bytes 1048576 | tf_op jit(solution)/shard_map/all_to_all | solution.py:214
  85.2 0.7 copy-done.6
  85.9 0.1 copy.23.bias_ref
  86.0 8.7 %all-to-all-done.2 = f32[4,32,1024]{2,1,0:T(8,128)S(1)} async-done(((f32[4,32,1024]{2,1,0:T(8,128)}), f32[4,32,1024]{2,1,0:T(8,128)S(1)}, u32[]{:S(2)}, u32[]{:S(2)}) %all-to-all-start.2) | async-done | bytes 524320 | tf_op jit(solution)/shard_map/all_to_all | solution.py:214
  94.7 1.0 layer_and_gradient.1
  95.7 9.3 %all_to_all.31 = f32[8,16,128]{2,1,0:T(8,128)S(1)} all-to-all(f32[8,16,128]{2,1,0:T(8,128)S(1)} %get-tuple-element.10), channel_id=1, replica_groups=mesh['z_far'=4,'z_near'=4,'y'=4,'core'=2,'feat'=4] {'y','core'}, dimensions={0} | all-to-all | bytes 131072 | tf_op jit(solution)/shard_map/all_to_all | solution.py:217
  105.1 14.5 %all_to_all.32 = f32[16,16,128]{2,1,0:T(8,128)S(1)} all-to-all(f32[16,16,128]{2,1,0:T(8,128)S(1)} %broadcast_in_dim.20), channel_id=1, replica_groups=mesh['z_far'=4,'z_near'=4,'y'=4,'core'=2,'feat'=4] {'z_far','z_near'}, dimensions={0} | all-to-all | bytes 262144 | tf_op jit(solution)/shard_map/all_to_all | solution.py:194
  119.7 10.8 %all_to_all.33 = f32[8,16,128]{2,1,0:T(8,128)S(1)} all-to-all(f32[8,16,128]{2,1,0:T(8,128)S(1)} %broadcast_in_dim.21), channel_id=1, replica_groups=mesh['z_far'=4,'z_near'=4,'y'=4,'core'=2,'feat'=4] {'y','core'}, dimensions={0} | all-to-all | bytes 131072 | tf_op jit(solution)/shard_map/all_to_all | solution.py:194
  130.5 0.1 slice_reduce_fusion
  130.6 0.6 reshape_squeeze.3
  131.2 0.6 slice_bitcast_fusion.1
  (17 shorter events, 0.2 us)
Async XLA Ops:
  0.6 0.7 copy-start.7
  1.4 0.9 copy-start.1
  2.3 0.8 copy-start.3
  36.9 15.2 %copy-start.5 = (bf16[32,256]{1,0:T(8,128)(2,1)S(1)}, bf16[32,256]{1,0:T(8,128)(2,1)}, u32[]{:S(2)}) copy-start(bf16[32,256]{1,0:T(8,128)(2,1)} %param.13) | copy-start | bytes 49156
  36.9 41.8 %copy-start = (bf16[32,128,128]{2,1,0:T(8,128)(2,1)S(1)}, bf16[32,128,128]{2,1,0:T(8,128)(2,1)}, u32[]{:S(2)}) copy-start(bf16[32,128,128]{2,1,0:T(8,128)(2,1)} %vals_ref.1) | copy-start | bytes 3145732
  36.9 41.7 %all-to-all-start.1 = ((bf16[32,128,128]{2,1,0:T(8,128)(2,1)}), bf16[32,128,128]{2,1,0:T(8,128)(2,1)S(1)}, u32[]{:S(2)}, u32[]{:S(2)}) async-start(bf16[32,128,128]{2,1,0:T(8,128)(2,1)} %bitcast.4), calls=%async_computation.1 | async-start | bytes 2097152 | tf_op jit(solution)/shard_map/all_to_all | solution.py:208
  78.6 0.7 copy-start.4
  81.1 13.6 %copy-start.2 = (bf16[1024,64]{0,1:T(8,128)(2,1)S(1)}, bf16[1024,64]{0,1:T(8,128)(2,1)}, u32[]{:S(2)}) copy-start(bf16[1024,64]{0,1:T(8,128)(2,1)} %param.15) | copy-start | bytes 393220
  81.1 13.6 %all-to-all-start.2 = ((f32[4,32,1024]{2,1,0:T(8,128)}), f32[4,32,1024]{2,1,0:T(8,128)S(1)}, u32[]{:S(2)}, u32[]{:S(2)}) async-start(f32[4,32,1024]{2,1,0:T(8,128)} %aggregate_tiles.1), calls=%async_computation.2 | async-start | bytes 1048576 | tf_op jit(solution)/shard_map/all_to_all | solution.py:214
  85.2 0.7 copy-start.6

commit v3 on v2

--- a/solution.py
+++ b/solution.py
@@ -19,13 +19,20 @@
 BF16 = jnp.bfloat16
 
 
+def as_column(row):
+    size = row.shape[1]
+    same = lax.broadcasted_iota(jnp.int32, (size, size), 0) == lax.broadcasted_iota(jnp.int32, (size, size), 1)
+    return jnp.sum(jnp.where(same, row, 0.0), axis=1, keepdims=True)
+
+
 def keep_kernel(keep_ref, features_ref, lists_ref, out_ref):
     planes, rows, block = out_ref.shape
-    kept = keep_ref.shape[0]
+    kept = keep_ref.shape[1]
     nodes = features_ref.shape[1]
     lists = lists_ref.shape[0] // planes
     lane = lax.broadcasted_iota(jnp.int32, (kept, features_ref.shape[0]), 1)
-    select = jnp.where(lane == keep_ref[...], 1.0, 0.0).astype(BF16)
+    wanted = as_column(keep_ref[...].astype(F32)).astype(jnp.int32)
+    select = jnp.where(lane == wanted, 1.0, 0.0).astype(BF16)
     columns = jnp.dot(select, features_ref[...], preferred_element_type=F32).astype(BF16)
     row = lists_ref[...]
     code = lax.shift_left(CODE + (row & (CODE - 1)), row // CODE)
@@ -47,9 +54,8 @@
         in_specs=[vmem] * 3,
         out_specs=vmem,
         out_shape=jax.ShapeDtypeStruct((planes, rows, block), BF16),
-        compiler_params=pltpu.CompilerParams(vmem_limit_bytes=24 << 20),
         name="keep_columns",
-    )(keep_cols[:, None], features, lists)
+    )(keep_cols[None, :], features, lists)
 
 
 def pick_kernel(held_ref, out_ref):
@@ -98,17 +104,15 @@
 
 
 def aggregate_kernel(tiles_row, cols_ref, own_ref, incoming_ref, vals_ref, out_ref):
-    kept, block = incoming_ref.shape[2:]
+    kept, block = incoming_ref.shape[1:]
     own = vals_ref.shape[0] // tiles_row
-    near = incoming_ref.shape[0]
     for tile in range(vals_ref.shape[0] // tiles_row):
         values, picked = [], []
         for term in range(tiles_row):
             at = tile * tiles_row + term
             column = cols_ref[at]
             mine = own_ref[pl.ds(pl.multiple_of(jnp.minimum(column, own - 1) * kept, kept), kept), :]
-            sender = jnp.maximum(column - own, 0)
-            theirs = incoming_ref[sender % near, sender // near]
+            theirs = incoming_ref[jnp.maximum(column - own, 0)]
             picked.append(jnp.where(column < own, mine, theirs))
             values.append(vals_ref[at])
         total = lax.dot_general(
@@ -119,7 +123,7 @@
 
 
 def aggregate(tile_cols, own, incoming, tile_vals, copies):
-    kept, block = incoming.shape[2:]
+    kept, block = incoming.shape[1:]
     tiles = own.shape[0] // kept
     vmem = pl.BlockSpec(memory_space=pltpu.VMEM)
     return pl.pallas_call(
@@ -138,6 +142,7 @@
     depth = agg_ref.shape[0]
     slope = math.sqrt(2.0 / math.pi)
     weight = jnp.concatenate([weight_ref[...]] * 3, axis=1)
+    bias = jnp.concatenate([bias_ref[...]] * (step // bias_ref.shape[1]), axis=1)
     grad_weight = jnp.zeros((hidden, depth), F32)
     grad_bias = jnp.zeros((hidden, 1), F32)
     for start in range(0, nodes, step):
@@ -147,7 +152,7 @@
         second = rest.astype(BF16)
         third = (rest - second.astype(F32)).astype(BF16)
         pre = jnp.dot(weight, jnp.concatenate([first, second, third], axis=0), preferred_element_type=F32)
-        pre = pre + bias_ref[...]
+        pre = pre + bias
         square = pre * pre
         bend = jnp.tanh(slope * (pre + 0.044715 * (pre * square)))
         half = 0.5 * (1.0 + bend)
@@ -166,10 +171,12 @@
         )
         grad_weight += (both[:hidden, depth:] + both[hidden:, :depth]) + both[:hidden, :depth]
     groups = terms_ref.shape[0]
-    terms_ref[:, : hidden // groups, :] = grad_weight.reshape(groups, hidden // groups, depth)
-    terms_ref[:, hidden // groups :, :] = jnp.broadcast_to(grad_bias, (hidden, depth)).reshape(
-        groups, hidden // groups, depth
-    )
+    rows = hidden // groups
+    lane = lax.broadcasted_iota(jnp.int32, (hidden, depth), 1)
+    spot = lax.broadcasted_iota(jnp.int32, (hidden, depth), 0)
+    diagonal = jnp.where(lane == spot, grad_bias, 0.0).reshape(groups, rows, depth)
+    terms_ref[:, :rows, :] = grad_weight.reshape(groups, rows, depth)
+    terms_ref[:, rows:, :] = jnp.broadcast_to(jnp.sum(diagonal, axis=1, keepdims=True), (groups, rows, depth))
 
 
 def layer(aggregated, weight, bias, grad_out, groups):
@@ -186,7 +193,28 @@
         ],
         compiler_params=pltpu.CompilerParams(vmem_limit_bytes=24 << 20),
         name="layer_and_gradient",
-    )(aggregated, weight, bias[:, None], grad_out)
+    )(aggregated, weight, bias, grad_out)
+
+
+def unpack_kernel(terms_ref, weight_ref, bias_ref):
+    groups = terms_ref.shape[0]
+    hidden, depth = weight_ref.shape
+    rows = hidden // groups
+    weight_ref[...] = terms_ref[:, :rows, :].reshape(hidden, depth)
+    bias_ref[...] = jnp.sum(terms_ref[:, rows : rows + 1, :], axis=0)[:, :hidden]
+
+
+def unpack(terms, hidden):
+    depth = terms.shape[2]
+    vmem = pl.BlockSpec(memory_space=pltpu.VMEM)
+    return pl.pallas_call(
+        unpack_kernel,
+        in_specs=[vmem],
+        out_specs=[vmem] * 2,
+        out_shape=[jax.ShapeDtypeStruct((hidden, depth), F32), jax.ShapeDtypeStruct((1, hidden), F32)],
+        compiler_params=pltpu.CompilerParams(vmem_limit_bytes=24 << 20),
+        name="unpack_gradients",
+    )(terms)
 
 
 def spread(array, axis):
@@ -206,20 +234,24 @@
     held = lax.all_to_all(outgoing, "z_far", 0, 0)
     picked = pick(held, near, kept).reshape(near, planes * kept, block)
     incoming = lax.all_to_all(picked, NEAR, 0, 0)
-    incoming = incoming.reshape(near, planes, kept, block)
+    incoming = incoming.reshape(near * planes, kept, block)
+    tiles = features.shape[0] // block
+    sender = tile_cols - tiles
+    place = tiles + lax.rem(sender, near) * planes + lax.div(sender, near)
+    tile_cols = jnp.where(sender < 0, tile_cols, place)
+    bias = jnp.broadcast_to(bias[:, None], (hidden, block))
     weight_all = lax.all_gather(weight, "feat", axis=0, tiled=True)
     columns = lax.dynamic_slice_in_dim(weight_all, lax.axis_index("feat") * hidden, hidden, 1).T
-    incoming, columns = lax.optimization_barrier((incoming, columns))
+    incoming, columns, tile_cols, bias = lax.optimization_barrier((incoming, columns, tile_cols, bias))
     aggregated = aggregate(tile_cols, own, incoming, tile_vals, feat)
     aggregated = lax.all_to_all(aggregated, "feat", 0, 0).reshape(feat * kept, -1)
     groups = lax.axis_size(PLANE)
     out, terms = layer(aggregated, columns, bias, grad_out.T, groups)
     terms = lax.all_to_all(terms, PLANE, 0, 0).sum(axis=0)
-    terms = spread(terms, RING).sum(axis=0)
-    terms = spread(terms, PLANE)
-    rows = hidden // groups
-    grad_weight = terms[:, :rows].reshape(hidden, feat * kept)
-    grad_bias = terms[:, rows:, 0]
+    rows = hidden // groups + 1
+    packed = spread(terms[:rows].reshape(1, -1), RING).sum(axis=0).reshape(rows, -1)
+    terms = spread(jnp.pad(packed, ((0, terms.shape[0] - rows), (0, 0))), PLANE)
+    grad_weight, grad_bias = unpack(terms, hidden)
     return out.T, grad_weight.T, grad_bias.reshape(hidden)
 
 

time: 132 us -> 128 us (0.970)
  blocking collectives: 74.9 us -> 86.8 us
  waiting for transfers between devices: 24.9 us -> 14.7 us
  starting transfers between devices: 19.3 us -> 15.2 us
  local copies, waits for them, and re-layouts: 5.38 us -> 1.72 us
  Pallas kernels: 6.56 us -> 7.97 us
    all_to_all x0 -> x1, blocking collectives: none -> 13.2 us  [shards(): lax.all_to_all(aggregated, 'feat', 0, 0).reshape(feat * kept, -1)]
    all_to_all x1 -> x0, waiting for transfers between devices: 8.68 us -> none  [shards(): lax.all_to_all(aggregated, 'feat', 0, 0).reshape(feat * kept, -1)]
    all_to_all x1 -> x0, starting transfers between devices: 4.14 us -> none  [shards(): lax.all_to_all(aggregated, 'feat', 0, 0).reshape(feat * kept, -1)]
    unnamed x17 -> x11, local copies, waits for them, and re-layouts: 3.79 us -> 0.66 us
    all_to_all x2, blocking collectives: 25.4 us -> 23.7 us  [spread(): lax.all_to_all(jnp.broadcast_to(array[None], (size,) + array.shape), axis...]
    pallas_call x1, Pallas kernels: 0.2 us -> 1.85 us  [keep(): pl.pallas_call(keep_kernel, in_specs=[vmem] * 3, out_specs=vmem, out_shap...]
    all_to_all x1, waiting for transfers between devices: 16.2 us -> 14.7 us  [shards(): incoming = lax.all_to_all(picked, NEAR, 0, 0)]
  transfers between devices with their start and end apart: 2 -> 1, of which waited for: 2 -> 1; matrix products, arithmetic and copies ran while one was open for 0% -> 1% of each run, Pallas kernels for 0% -> 0%
where the time goes in v3:
time: 128 us; the launch traced here: 127 us
  blocking collectives  86.8 us (68%)
  starting transfers between devices  15.2 us (12%)
  waiting for transfers between devices  14.7 us (11%)
  Pallas kernels  7.97 us (6%)
  local copies, waits for them, and re-layouts  1.72 us (1%)
    all_to_all x1, blocking collectives, shards(): held = lax.all_to_all(outgoing, 'z_far', 0, 0)  30.2 us
    all_to_all x2, blocking collectives, spread(): lax.all_to_all(jnp.broadcast_to(array[None], (size,) + array.shape), axis...  23.7 us
    all_to_all x1, starting transfers between devices, shards(): incoming = lax.all_to_all(picked, NEAR, 0, 0)  15.2 us
    all_to_all x1, waiting for transfers between devices, shards(): incoming = lax.all_to_all(picked, NEAR, 0, 0)  14.7 us
    all_to_all x1, blocking collectives, shards(): lax.all_to_all(aggregated, 'feat', 0, 0).reshape(feat * kept, -1)  13.2 us
    all_gather x1, blocking collectives, shards(): weight_all = lax.all_gather(weight, 'feat', axis=0, tiled=True)  10.2 us
    all_to_all x1, blocking collectives, shards(): terms = lax.all_to_all(terms, PLANE, 0, 0).sum(axis=0)  9.55 us
    pallas_call x1, Pallas kernels, pick(): pl.pallas_call(pick_kernel, grid=(planes,), in_specs=[pl.BlockSpec((1, ro...  3.46 us
  transfers between devices with their start and end apart: 1, of which 1 were waited for; matrix products, arithmetic and copies ran while one was open for 1% of the time, Pallas kernels for 0%

profile of v3, /device:TPU:1, one launch (start us, length us, event | category | flops | bytes accessed | tf_op | source)
XLA Modules:
  0.0 127.3 jit_solution(915657639825499115)
XLA Ops:
  0.6 1.9 %keep_columns.1 = bf16[4,288,128]{2,1,0:T(8,128)(2,1)} custom-call(s32[1,32]{1,0:T(1,128)} %bitcast.23, bf16[64,1024]{1,0:T(8,128)(2,1)} %bitcast.20, s32[128,128]{1,0:T(8,128)} %bitcast.21), custom_call_target="tpu_custom_call" | custom-call | tf_op jit(solution)/shard_map/keep_columns/pallas_call | solution.py:52
  2.5 30.2 %all_to_all.30.held_ref = bf16[4,288,128]{2,1,0:T(8,128)(2,1)S(1)} all-to-all(bf16[4,288,128]{2,1,0:T(8,128)(2,1)} %keep_columns.1), channel_id=1, replica_groups=mesh['z_far'=4,'z_near'=4,'y'=4,'core'=2,'feat'=4] {'z_far'}, dimensions={0} | all-to-all | bytes 589824 | tf_op jit(solution)/shard_map/all_to_all | solution.py:234
  32.7 3.5 %pick_rows.1 = bf16[32,4,32,128]{3,2,1,0:T(8,128)(2,1)} custom-call(bf16[4,288,128]{2,1,0:T(8,128)(2,1)S(1)} %all_to_all.30.held_ref), custom_call_target="tpu_custom_call" | custom-call | tf_op jit(solution)/shard_map/pick_rows/pallas_call | solution.py:95
  36.2 15.2 %all-to-all-start.1 = ((bf16[32,128,128]{2,1,0:T(8,128)(2,1)}), bf16[32,128,128]{2,1,0:T(8,128)(2,1)S(1)}, u32[]{:S(2)}, u32[]{:S(2)}) async-start(bf16[32,128,128]{2,1,0:T(8,128)(2,1)} %bitcast.3), calls=%async_computation.1 | async-start | bytes 2097152 | tf_op jit(solution)/shard_map/all_to_all | solution.py:236
  51.3 0.0 copy-done.2
  51.3 10.2 %all_gather.3 = bf16[128,256]{1,0:T(8,128)(2,1)S(1)} all-gather(bf16[32,256]{1,0:T(8,128)(2,1)S(1)} %copy-done.2), channel_id=1, replica_groups=mesh['z_far'=4,'z_near'=4,'y'=4,'core'=2,'feat'=4] {'feat'}, dimensions={0}, use_global_device_ids=true | all-gather | bytes 81920 | tf_op jit(solution)/shard_map/all_gather | solution.py:243
  61.6 0.1 constant_dynamic-slice_fusion
  61.6 0.0 copy-start.4
  61.7 0.1 copy.17
  61.7 0.6 copy-done.4
  62.3 0.9 slice_bitcast_fusion.own_ref
  63.2 14.7 %all-to-all-done.1 = bf16[32,128,128]{2,1,0:T(8,128)(2,1)S(1)} async-done(((bf16[32,128,128]{2,1,0:T(8,128)(2,1)}), bf16[32,128,128]{2,1,0:T(8,128)(2,1)S(1)}, u32[]{:S(2)}, u32[]{:S(2)}) %all-to-all-start.1) | async-done | bytes 1048608 | tf_op jit(solution)/shard_map/all_to_all | solution.py:236
  77.9 0.0 copy-done.3
  77.9 0.1 broadcast_in_dim.11.bias_ref
  78.0 0.0 copy-done
  78.0 1.0 aggregate_tiles.1
  79.0 0.0 copy-start.1
  79.0 13.2 %all_to_all.31 = f32[4,32,1024]{2,1,0:T(8,128)S(1)} all-to-all(f32[4,32,1024]{2,1,0:T(8,128)S(1)} %aggregate_tiles.1), channel_id=1, replica_groups=mesh['z_far'=4,'z_near'=4,'y'=4,'core'=2,'feat'=4] {'feat'}, dimensions={0} | all-to-all | bytes 1048576 | tf_op jit(solution)/shard_map/all_to_all | solution.py:247
  92.2 1.0 layer_and_gradient.1
  93.2 9.6 %all_to_all.32 = f32[8,16,128]{2,1,0:T(8,128)S(1)} all-to-all(f32[8,16,128]{2,1,0:T(8,128)S(1)} %get-tuple-element.16), channel_id=1, replica_groups=mesh['z_far'=4,'z_near'=4,'y'=4,'core'=2,'feat'=4] {'y','core'}, dimensions={0} | all-to-all | bytes 131072 | tf_op jit(solution)/shard_map/all_to_all | solution.py:250
  102.9 14.2 %all_to_all.33 = f32[16,1,1152]{2,1,0:T(1,128)S(1)} all-to-all(f32[16,1,1152]{2,1,0:T(1,128)S(1)} %broadcast_in_dim.25), channel_id=1, replica_groups=mesh['z_far'=4,'z_near'=4,'y'=4,'core'=2,'feat'=4] {'z_far','z_near'}, dimensions={0} | all-to-all | bytes 147456 | tf_op jit(solution)/shard_map/all_to_all | solution.py:222
  117.1 0.1 reduce_sum.19
  117.2 9.5 %all_to_all.34.terms_ref = f32[8,16,128]{2,1,0:T(8,128)S(1)} all-to-all(f32[8,16,128]{2,1,0:T(8,128)S(1)} %broadcast_in_dim.26), channel_id=1, replica_groups=mesh['z_far'=4,'z_near'=4,'y'=4,'core'=2,'feat'=4] {'y','core'}, dimensions={0} | all-to-all | bytes 131072 | tf_op jit(solution)/shard_map/all_to_all | solution.py:222
  126.6 0.6 unpack_gradients.1
  (10 shorter events, 0.1 us)
Async XLA Ops:
  36.2 15.2 %copy-start.2 = (bf16[32,256]{1,0:T(8,128)(2,1)S(1)}, bf16[32,256]{1,0:T(8,128)(2,1)}, u32[]{:S(2)}) copy-start(bf16[32,256]{1,0:T(8,128)(2,1)} %param.13) | copy-start | bytes 49156
  36.2 41.8 %copy-start = (bf16[32,128,128]{2,1,0:T(8,128)(2,1)S(1)}, bf16[32,128,128]{2,1,0:T(8,128)(2,1)}, u32[]{:S(2)}) copy-start(bf16[32,128,128]{2,1,0:T(8,128)(2,1)} %vals_ref.1) | copy-start | bytes 3145732
  36.2 41.8 %all-to-all-start.1 = ((bf16[32,128,128]{2,1,0:T(8,128)(2,1)}), bf16[32,128,128]{2,1,0:T(8,128)(2,1)S(1)}, u32[]{:S(2)}, u32[]{:S(2)}) async-start(bf16[32,128,128]{2,1,0:T(8,128)(2,1)} %bitcast.3), calls=%async_computation.1 | async-start | bytes 2097152 | tf_op jit(solution)/shard_map/all_to_all | solution.py:236
  61.6 0.7 copy-start.4
  62.3 15.6 %copy-start.3 = (f32[64]{0:T(128)S(1)}, f32[64]{0:T(128)}, u32[]{:S(2)}) copy-start(f32[64]{0:T(128)} %param.14) | copy-start | bytes 772
  79.0 13.2 %copy-start.1 = (bf16[1024,64]{0,1:T(8,128)(2,1)S(1)}, bf16[1024,64]{0,1:T(8,128)(2,1)}, u32[]{:S(2)}) copy-start(bf16[1024,64]{0,1:T(8,128)(2,1)} %param.15) | copy-start | bytes 393220

commit v4 on v3

--- a/solution.py
+++ b/solution.py
@@ -15,6 +15,7 @@
 NT = (((1,), (1,)), ((), ()))
 LOW = 256
 CODE = 128
+ORDER = (2, 1, 3)
 F32 = jnp.float32
 BF16 = jnp.bfloat16
 
@@ -25,8 +26,10 @@
     return jnp.sum(jnp.where(same, row, 0.0), axis=1, keepdims=True)
 
 
-def keep_kernel(keep_ref, features_ref, lists_ref, out_ref):
-    planes, rows, block = out_ref.shape
+def keep_kernel(keep_ref, features_ref, lists_ref, *refs):
+    out_refs, code_ref = refs[:-1], refs[-1]
+    planes = len(out_refs)
+    rows, block = out_refs[0].shape
     kept = keep_ref.shape[1]
     nodes = features_ref.shape[1]
     lists = lists_ref.shape[0] // planes
@@ -36,11 +39,13 @@
     columns = jnp.dot(select, features_ref[...], preferred_element_type=F32).astype(BF16)
     row = lists_ref[...]
     code = lax.shift_left(CODE + (row & (CODE - 1)), row // CODE)
-    code = (code.astype(F32) * (1.0 / CODE)).astype(BF16)
-    for plane in range(planes):
+    code_ref[...] = (code.astype(F32) * (1.0 / CODE)).astype(BF16)
+    me = lax.axis_index("z_far")
+    for ahead, out_ref in enumerate(out_refs):
         for tile in range(nodes // block):
-            out_ref[plane, tile * kept : (tile + 1) * kept, :] = columns[:, tile * block : (tile + 1) * block]
-        out_ref[plane, rows - lists :, :] = code[plane * lists : (plane + 1) * lists]
+            out_ref[tile * kept : (tile + 1) * kept, :] = columns[:, tile * block : (tile + 1) * block]
+        first = pl.multiple_of(lax.rem(me + ahead, planes) * lists, lists)
+        out_ref[rows - lists :, :] = code_ref[pl.ds(first, lists), :]
 
 
 def keep(keep_cols, features, lists, planes):
@@ -52,35 +57,37 @@
     return pl.pallas_call(
         keep_kernel,
         in_specs=[vmem] * 3,
-        out_specs=vmem,
-        out_shape=jax.ShapeDtypeStruct((planes, rows, block), BF16),
+        out_specs=[vmem] * planes,
+        out_shape=[jax.ShapeDtypeStruct((rows, block), BF16)] * planes,
+        scratch_shapes=[pltpu.VMEM(lists.shape, BF16)],
         name="keep_columns",
     )(keep_cols[None, :], features, lists)
 
 
-def pick_kernel(held_ref, out_ref):
+def pick_kernel(held_ref, *rest):
+    out_ref = rest[-1]
     lists, _, kept, block = out_ref.shape
-    tiles = (held_ref.shape[1] - lists) // kept
+    tiles = (held_ref.shape[0] - lists) // kept
     span = LOW // block
     highs = tiles // span
     table = jnp.concatenate(
         [
-            jnp.concatenate([held_ref[0, t * kept : (t + 1) * kept, :] for t in range(h * span, (h + 1) * span)], axis=1)
+            jnp.concatenate([held_ref[t * kept : (t + 1) * kept, :] for t in range(h * span, (h + 1) * span)], axis=1)
             for h in range(highs)
         ],
         axis=0,
     )
-    code = (held_ref[0, tiles * kept :, :].astype(F32) * CODE).astype(jnp.int32)
+    code = (held_ref[tiles * kept :, :].astype(F32) * CODE).astype(jnp.int32)
     shift = jnp.zeros((lists, block), jnp.int32)
     for step in range(1, tiles + 1):
         shift += jnp.where(code >= CODE << step, 1, 0)
     row = shift * CODE + (lax.shift_right_logical(code, shift) - CODE)
-    sub = lax.broadcasted_iota(jnp.int32, (LOW, 2 * block), 0)
+    sub = lax.broadcasted_iota(jnp.int32, (LOW, 2 * block), 0).astype(F32).astype(BF16)
     for pair in range(lists // 2):
         rows = jnp.concatenate([row[2 * pair : 2 * pair + 1, :], row[2 * pair + 1 : 2 * pair + 2, :]], axis=1)
-        low = rows & (LOW - 1)
+        low = (rows & (LOW - 1)).astype(F32).astype(BF16)
         high = rows // LOW
-        onehot = jnp.where(sub == low, 1.0, 0.0).astype(BF16)
+        onehot = jnp.where(sub == low, jnp.ones((), BF16), jnp.zeros((), BF16))
         found = jnp.dot(table, onehot, preferred_element_type=F32)
         total = jnp.zeros((kept, 2 * block), F32)
         for step in range(highs):
@@ -90,17 +97,23 @@
         out_ref[2 * pair + 1, 0] = total[:, block:]
 
 
-def pick(held, lists, kept):
-    planes, rows, block = held.shape
+def pick(held, part, parts, lists, kept, before):
+    rows, block = held.shape
+    earlier = [] if before is None else [before]
     return pl.pallas_call(
         pick_kernel,
-        grid=(planes,),
-        in_specs=[pl.BlockSpec((1, rows, block), lambda i: (i, 0, 0))],
-        out_specs=pl.BlockSpec((lists, 1, kept, block), lambda i: (0, i, 0, 0)),
-        out_shape=jax.ShapeDtypeStruct((lists, planes, kept, block), BF16),
-        compiler_params=pltpu.CompilerParams(vmem_limit_bytes=24 << 20),
+        grid=(1,),
+        in_specs=[pl.BlockSpec((rows, block), lambda i: (0, 0))]
+        + [pl.BlockSpec(memory_space=pl.ANY)] * len(earlier),
+        out_specs=pl.BlockSpec((lists, 1, kept, block), lambda i: (0, part, 0, 0)),
+        out_shape=jax.ShapeDtypeStruct((lists, parts, kept, block), BF16),
+        input_output_aliases={1: 0} if earlier else {},
+        compiler_params=pltpu.CompilerParams(vmem_limit_bytes=24 << 20),
+        cost_estimate=pl.CostEstimate(
+            flops=2 * lists * block * LOW * block, bytes_accessed=2 * block * (lists * kept + rows), transcendentals=0
+        ),
         name="pick_rows",
-    )(held)
+    )(held, *earlier)
 
 
 def aggregate_kernel(tiles_row, cols_ref, own_ref, incoming_ref, vals_ref, out_ref):
@@ -230,14 +243,20 @@
     near = lax.axis_size(NEAR)
     block = send_rows.shape[2]
     outgoing = keep(keep_cols, features.T, send_rows[0], planes)
-    own = outgoing[0, : features.shape[0] // block * kept]
-    held = lax.all_to_all(outgoing, "z_far", 0, 0)
-    picked = pick(held, near, kept).reshape(near, planes * kept, block)
+    own = outgoing[0][: features.shape[0] // block * kept]
+    held = [outgoing[0]] + [None] * (planes - 1)
+    for ahead in ORDER:
+        held[ahead] = lax.ppermute(outgoing[ahead], "z_far", [(i, (i + ahead) % planes) for i in range(planes)])
+    picked = None
+    for ahead in (0,) + ORDER:
+        picked = pick(held[ahead], ahead, planes, near, kept, picked)
+    picked = picked.reshape(near, planes * kept, block)
     incoming = lax.all_to_all(picked, NEAR, 0, 0)
     incoming = incoming.reshape(near * planes, kept, block)
     tiles = features.shape[0] // block
     sender = tile_cols - tiles
-    place = tiles + lax.rem(sender, near) * planes + lax.div(sender, near)
+    behind = lax.rem(lax.axis_index("z_far") + planes - lax.div(sender, near), planes)
+    place = tiles + lax.rem(sender, near) * planes + behind
     tile_cols = jnp.where(sender < 0, tile_cols, place)
     bias = jnp.broadcast_to(bias[:, None], (hidden, block))
     weight_all = lax.all_gather(weight, "feat", axis=0, tiled=True)

time: 128 us -> 125 us (0.977)
  blocking collectives: 86.8 us -> 60.6 us
  starting transfers between devices: 15.2 us -> 33.6 us
  waiting for transfers between devices: 14.7 us -> 17.1 us
  local copies, waits for them, and re-layouts: 1.72 us -> 3.2 us
  Pallas kernels: 7.97 us -> 9.45 us
    all_to_all x1 -> x0, blocking collectives: 30.2 us -> none  [shards(): held = lax.all_to_all(outgoing, 'z_far', 0, 0)]
    ppermute x0 -> x3, starting transfers between devices: none -> 25.4 us  [shards(): lax.ppermute(outgoing[ahead], 'z_far', [(i, (i + ahead) % planes) for i i...]
    all_to_all x1, starting transfers between devices: 15.2 us -> 8.11 us  [shards(): incoming = lax.all_to_all(picked, NEAR, 0, 0)]
    all_to_all x2, blocking collectives: 23.7 us -> 27.7 us  [spread(): lax.all_to_all(jnp.broadcast_to(array[None], (size,) + array.shape), axis...]
    unnamed x11 -> x15, local copies, waits for them, and re-layouts: 0.66 us -> 2.98 us
    ppermute x0 -> x3, waiting for transfers between devices: none -> 2.26 us  [shards(): lax.ppermute(outgoing[ahead], 'z_far', [(i, (i + ahead) % planes) for i i...]
    pallas_call x2 -> x5, Pallas kernels: 5.31 us -> 6.8 us  [the longest x4 4.94 us: pick(): pl.pallas_call(pick_kernel, grid=(1,), in_specs=[pl.BlockSpec((rows, bloc...]
  transfers between devices with their start and end apart: 1 -> 4, of which waited for: 1 -> 2; matrix products, arithmetic and copies ran while one was open for 1% -> 0% of each run, Pallas kernels for 0% -> 3%
where the time goes in v4:
time: 125 us
  blocking collectives  60.6 us (48%)
  starting transfers between devices  33.6 us (27%)
  waiting for transfers between devices  17.1 us (14%)
  Pallas kernels  9.45 us (8%)
  local copies, waits for them, and re-layouts  3.2 us (3%)
    all_to_all x2, blocking collectives, spread(): lax.all_to_all(jnp.broadcast_to(array[None], (size,) + array.shape), axis...  27.7 us
    ppermute x3, starting transfers between devices, shards(): lax.ppermute(outgoing[ahead], 'z_far', [(i, (i + ahead) % planes) for i i...  25.4 us
    all_to_all x1, waiting for transfers between devices, shards(): incoming = lax.all_to_all(picked, NEAR, 0, 0)  14.8 us
    all_to_all x1, blocking collectives, shards(): lax.all_to_all(aggregated, 'feat', 0, 0).reshape(feat * kept, -1)  13.2 us
    all_gather x1, blocking collectives, shards(): weight_all = lax.all_gather(weight, 'feat', axis=0, tiled=True)  10.2 us
    all_to_all x1, blocking collectives, shards(): terms = lax.all_to_all(terms, PLANE, 0, 0).sum(axis=0)  9.55 us
    all_to_all x1, starting transfers between devices, shards(): incoming = lax.all_to_all(picked, NEAR, 0, 0)  8.11 us
    pallas_call x4, Pallas kernels, pick(): pl.pallas_call(pick_kernel, grid=(1,), in_specs=[pl.BlockSpec((rows, bloc...  4.94 us
  transfers between devices with their start and end apart: 4, of which 2 were waited for; matrix products, arithmetic and copies ran while one was open for 0% of the time, Pallas kernels for 3%

profile of v4, /device:TPU:1, one launch (start us, length us, event | category | flops | bytes accessed | tf_op | source)
XLA Modules:
  0.0 124.8 jit_solution(14611260171430623872)
XLA Ops:
  0.6 1.9 %keep_columns.1 = (bf16[288,128]{1,0:T(8,128)(2,1)}, bf16[288,128]{1,0:T(8,128)(2,1)}, bf16[288,128]{1,0:T(8,128)(2,1)}, bf16[288,128]{1,0:T(8,128)(2,1)}) custom-call(s32[1,32]{1,0:T(1,128)} %bitcast.21, bf16[64,1024]{1,0:T(8,128)(2,1)} %bitcast.18, s32[128,128]{1,0:T(8,128)} %bitcast.19), custom_call_target="tpu_custom_call" | custom-call | tf_op jit(solution)/shard_map/keep_columns/pallas_call | solution.py:57
  2.5 16.3 %collective-permute-start.2 = (bf16[288,128]{1,0:T(8,128)(2,1)}, bf16[288,128]{1,0:T(8,128)(2,1)S(1)}, u32[]{:S(2)}, u32[]{:S(2)}) collective-permute-start(bf16[288,128]{1,0:T(8,128)(2,1)} %get-tuple-element.17), channel_id=1, source_target_pairs={{0,256},{128,384},{256,0},{384,128},{1,257},{129,385},{257,1},{385... | collective-permute-start | bytes 221192 | tf_op jit(solution)/shard_map/ppermute | solution.py:249
  18.8 4.0 %collective-permute-start.1 = (bf16[288,128]{1,0:T(8,128)(2,1)}, bf16[288,128]{1,0:T(8,128)(2,1)S(1)}, u32[]{:S(2)}, u32[]{:S(2)}) collective-permute-start(bf16[288,128]{1,0:T(8,128)(2,1)} %get-tuple-element.16), channel_id=1, source_target_pairs={{0,128},{128,256},{256,384},{384,0},{1,129},{129,257},{257,385},{3... | collective-permute-start | bytes 221192 | tf_op jit(solution)/shard_map/ppermute | solution.py:249
  22.8 5.2 %collective-permute-start = (bf16[288,128]{1,0:T(8,128)(2,1)}, bf16[288,128]{1,0:T(8,128)(2,1)S(1)}, u32[]{:S(2)}, u32[]{:S(2)}) collective-permute-start(bf16[288,128]{1,0:T(8,128)(2,1)} %get-tuple-element.15), channel_id=1, source_target_pairs={{0,384},{128,0},{256,128},{384,256},{1,385},{129,1},{257,129},{385... | collective-permute-start | bytes 221192 | tf_op jit(solution)/shard_map/ppermute | solution.py:249
  28.0 0.9 copy-done.1
  28.8 1.2 pick_rows.4.rest_0_
  30.1 1.2 %pick_rows.5.rest_0_ = bf16[32,4,32,128]{3,2,1,0:T(8,128)(2,1)} custom-call(bf16[288,128]{1,0:T(8,128)(2,1)S(1)} %collective-permute-done.2.held_ref, bf16[32,4,32,128]{3,2,1,0:T(8,128)(2,1)} %pick_rows.4.rest_0_), custom_call_target="tpu_custom_call", output_to_operand_aliasing={{}: (1, {})} | custom-call | flops 268435456 | bytes 335872 | tf_op jit(solution)/shard_map/pick_rows/pallas_call | solution.py:103
  31.3 1.3 %pick_rows.6.rest_0_ = bf16[32,4,32,128]{3,2,1,0:T(8,128)(2,1)} custom-call(bf16[288,128]{1,0:T(8,128)(2,1)S(1)} %collective-permute-done.1.held_ref, bf16[32,4,32,128]{3,2,1,0:T(8,128)(2,1)} %pick_rows.5.rest_0_), custom_call_target="tpu_custom_call", output_to_operand_aliasing={{}: (1, {})} | custom-call | flops 268435456 | bytes 335872 | tf_op jit(solution)/shard_map/pick_rows/pallas_call | solution.py:103
  32.6 2.3 %collective-permute-done.held_ref = bf16[288,128]{1,0:T(8,128)(2,1)S(1)} collective-permute-done((bf16[288,128]{1,0:T(8,128)(2,1)}, bf16[288,128]{1,0:T(8,128)(2,1)S(1)}, u32[]{:S(2)}, u32[]{:S(2)}) %collective-permute-start) | collective-permute-done | bytes 73760 | tf_op jit(solution)/shard_map/ppermute | solution.py:249
  34.8 1.2 pick_rows.7
  36.1 8.1 %all-to-all-start = ((bf16[32,128,128]{2,1,0:T(8,128)(2,1)}), bf16[32,128,128]{2,1,0:T(8,128)(2,1)S(1)}, u32[]{:S(2)}, u32[]{:S(2)}) async-start(bf16[32,128,128]{2,1,0:T(8,128)(2,1)} %bitcast.3), calls=%async_computation | async-start | bytes 2097152 | tf_op jit(solution)/shard_map/all_to_all | solution.py:254
  44.2 0.7 copy-done.4
  44.9 10.2 %all_gather.3 = bf16[128,256]{1,0:T(8,128)(2,1)S(1)} all-gather(bf16[32,256]{1,0:T(8,128)(2,1)S(1)} %copy-done.4), channel_id=1, replica_groups=mesh['z_far'=4,'z_near'=4,'y'=4,'core'=2,'feat'=4] {'feat'}, dimensions={0}, use_global_device_ids=true | all-gather | bytes 81920 | tf_op jit(solution)/shard_map/all_gather | solution.py:262
  55.2 0.1 copy.20
  55.3 0.7 copy-done.6
  56.0 14.8 %all-to-all-done = bf16[32,128,128]{2,1,0:T(8,128)(2,1)S(1)} async-done(((bf16[32,128,128]{2,1,0:T(8,128)(2,1)}), bf16[32,128,128]{2,1,0:T(8,128)(2,1)S(1)}, u32[]{:S(2)}, u32[]{:S(2)}) %all-to-all-start) | async-done | bytes 1048608 | tf_op jit(solution)/shard_map/all_to_all | solution.py:254
  70.8 0.7 copy-done.5
  71.5 1.0 aggregate_tiles.1
  72.5 13.2 %all_to_all.25 = f32[4,32,1024]{2,1,0:T(8,128)S(1)} all-to-all(f32[4,32,1024]{2,1,0:T(8,128)S(1)} %aggregate_tiles.1), channel_id=1, replica_groups=mesh['z_far'=4,'z_near'=4,'y'=4,'core'=2,'feat'=4] {'feat'}, dimensions={0} | all-to-all | bytes 1048576 | tf_op jit(solution)/shard_map/all_to_all | solution.py:266
  85.7 1.0 layer_and_gradient.1
  86.7 9.6 %all_to_all.26 = f32[8,16,128]{2,1,0:T(8,128)S(1)} all-to-all(f32[8,16,128]{2,1,0:T(8,128)S(1)} %get-tuple-element.24), channel_id=1, replica_groups=mesh['z_far'=4,'z_near'=4,'y'=4,'core'=2,'feat'=4] {'y','core'}, dimensions={0} | all-to-all | bytes 131072 | tf_op jit(solution)/shard_map/all_to_all | solution.py:269
  96.3 18.3 %all_to_all.27 = f32[16,1,1152]{2,1,0:T(1,128)S(1)} all-to-all(f32[16,1,1152]{2,1,0:T(1,128)S(1)} %broadcast_in_dim.25), channel_id=1, replica_groups=mesh['z_far'=4,'z_near'=4,'y'=4,'core'=2,'feat'=4] {'z_far','z_near'}, dimensions={0} | all-to-all | bytes 147456 | tf_op jit(solution)/shard_map/all_to_all | solution.py:235
  114.7 9.4 %all_to_all.28.terms_ref = f32[8,16,128]{2,1,0:T(8,128)S(1)} all-to-all(f32[8,16,128]{2,1,0:T(8,128)S(1)} %broadcast_in_dim.26), channel_id=1, replica_groups=mesh['z_far'=4,'z_near'=4,'y'=4,'core'=2,'feat'=4] {'y','core'}, dimensions={0} | all-to-all | bytes 131072 | tf_op jit(solution)/shard_map/all_to_all | solution.py:235
  124.1 0.6 unpack_gradients.1
  (22 shorter events, 0.3 us)
Async XLA Ops:
  2.5 27.6 %collective-permute-start.2 = (bf16[288,128]{1,0:T(8,128)(2,1)}, bf16[288,128]{1,0:T(8,128)(2,1)S(1)}, u32[]{:S(2)}, u32[]{:S(2)}) collective-permute-start(bf16[288,128]{1,0:T(8,128)(2,1)} %get-tuple-element.17), channel_id=1, source_target_pairs={{0,256},{128,384},{256,0},{384,128},{1,257},{129,385},{257,1},{385... | collective-permute-start | bytes 221192 | tf_op jit(solution)/shard_map/ppermute | solution.py:249
  18.8 12.6 %collective-permute-start.1 = (bf16[288,128]{1,0:T(8,128)(2,1)}, bf16[288,128]{1,0:T(8,128)(2,1)S(1)}, u32[]{:S(2)}, u32[]{:S(2)}) collective-permute-start(bf16[288,128]{1,0:T(8,128)(2,1)} %get-tuple-element.16), channel_id=1, source_target_pairs={{0,128},{128,256},{256,384},{384,0},{1,129},{129,257},{257,385},{3... | collective-permute-start | bytes 221192 | tf_op jit(solution)/shard_map/ppermute | solution.py:249
  22.8 12.1 %collective-permute-start = (bf16[288,128]{1,0:T(8,128)(2,1)}, bf16[288,128]{1,0:T(8,128)(2,1)S(1)}, u32[]{:S(2)}, u32[]{:S(2)}) collective-permute-start(bf16[288,128]{1,0:T(8,128)(2,1)} %get-tuple-element.15), channel_id=1, source_target_pairs={{0,384},{128,0},{256,128},{384,256},{1,385},{129,1},{257,129},{385... | collective-permute-start | bytes 221192 | tf_op jit(solution)/shard_map/ppermute | solution.py:249
  28.0 0.9 copy-start.1
  36.0 8.1 %copy-start.2 = (bf16[288,128]{1,0:T(8,128)(2,1)S(1)}, bf16[288,128]{1,0:T(8,128)(2,1)}, u32[]{:S(2)}) copy-start(bf16[288,128]{1,0:T(8,128)(2,1)} %get-tuple-element.18.held_ref) | copy-start | bytes 221188
  36.1 35.4 %copy-start = (bf16[32,128,128]{2,1,0:T(8,128)(2,1)S(1)}, bf16[32,128,128]{2,1,0:T(8,128)(2,1)}, u32[]{:S(2)}) copy-start(bf16[32,128,128]{2,1,0:T(8,128)(2,1)} %vals_ref.1) | copy-start | bytes 3145732
  36.1 34.7 %all-to-all-start = ((bf16[32,128,128]{2,1,0:T(8,128)(2,1)}), bf16[32,128,128]{2,1,0:T(8,128)(2,1)S(1)}, u32[]{:S(2)}, u32[]{:S(2)}) async-start(bf16[32,128,128]{2,1,0:T(8,128)(2,1)} %bitcast.3), calls=%async_computation | async-start | bytes 2097152 | tf_op jit(solution)/shard_map/all_to_all | solution.py:254
  44.2 0.7 copy-start.4
  55.3 0.7 copy-start.6
  70.8 0.7 copy-start.5
  72.5 13.2 %copy-start.3 = (bf16[1024,64]{0,1:T(8,128)(2,1)S(1)}, bf16[1024,64]{0,1:T(8,128)(2,1)}, u32[]{:S(2)}) copy-start(bf16[1024,64]{0,1:T(8,128)(2,1)} %param.15) | copy-start | bytes 393220

commit v5 on v4

--- a/solution.py
+++ b/solution.py
@@ -149,13 +149,13 @@
     )(tile_cols, own, incoming, tile_vals)
 
 
-def layer_kernel(agg_ref, weight_ref, bias_ref, grad_ref, out_ref, terms_ref):
+def layer_kernel(agg_ref, weight_ref, grad_ref, out_ref, terms_ref):
     hidden, nodes = grad_ref.shape
     step = 256
     depth = agg_ref.shape[0]
     slope = math.sqrt(2.0 / math.pi)
-    weight = jnp.concatenate([weight_ref[...]] * 3, axis=1)
-    bias = jnp.concatenate([bias_ref[...]] * (step // bias_ref.shape[1]), axis=1)
+    weight = jnp.concatenate([weight_ref[:, :depth].astype(BF16)] * 3, axis=1)
+    bias = jnp.concatenate([weight_ref[:, depth:]] * (step // depth), axis=1)
     grad_weight = jnp.zeros((hidden, depth), F32)
     grad_bias = jnp.zeros((hidden, 1), F32)
     for start in range(0, nodes, step):
@@ -192,13 +192,13 @@
     terms_ref[:, rows:, :] = jnp.broadcast_to(jnp.sum(diagonal, axis=1, keepdims=True), (groups, rows, depth))
 
 
-def layer(aggregated, weight, bias, grad_out, groups):
+def layer(aggregated, weight, grad_out, groups):
     depth, nodes = aggregated.shape
     hidden = weight.shape[0]
     vmem = pl.BlockSpec(memory_space=pltpu.VMEM)
     return pl.pallas_call(
         layer_kernel,
-        in_specs=[vmem] * 4,
+        in_specs=[vmem] * 3,
         out_specs=[vmem] * 2,
         out_shape=[
             jax.ShapeDtypeStruct((hidden, nodes), BF16),
@@ -206,7 +206,7 @@
         ],
         compiler_params=pltpu.CompilerParams(vmem_limit_bytes=24 << 20),
         name="layer_and_gradient",
-    )(aggregated, weight, bias, grad_out)
+    )(aggregated, weight, grad_out)
 
 
 def unpack_kernel(terms_ref, weight_ref, bias_ref):
@@ -258,14 +258,15 @@
     behind = lax.rem(lax.axis_index("z_far") + planes - lax.div(sender, near), planes)
     place = tiles + lax.rem(sender, near) * planes + behind
     tile_cols = jnp.where(sender < 0, tile_cols, place)
-    bias = jnp.broadcast_to(bias[:, None], (hidden, block))
     weight_all = lax.all_gather(weight, "feat", axis=0, tiled=True)
     columns = lax.dynamic_slice_in_dim(weight_all, lax.axis_index("feat") * hidden, hidden, 1).T
-    incoming, columns, tile_cols, bias = lax.optimization_barrier((incoming, columns, tile_cols, bias))
+    bias = jnp.broadcast_to(bias[:, None], columns.shape)
+    columns = jnp.concatenate([columns.astype(F32), bias], axis=1)
+    incoming, columns, tile_cols = lax.optimization_barrier((incoming, columns, tile_cols))
     aggregated = aggregate(tile_cols, own, incoming, tile_vals, feat)
     aggregated = lax.all_to_all(aggregated, "feat", 0, 0).reshape(feat * kept, -1)
     groups = lax.axis_size(PLANE)
-    out, terms = layer(aggregated, columns, bias, grad_out.T, groups)
+    out, terms = layer(aggregated, columns, grad_out.T, groups)
     terms = lax.all_to_all(terms, PLANE, 0, 0).sum(axis=0)
     rows = hidden // groups + 1
     packed = spread(terms[:rows].reshape(1, -1), RING).sum(axis=0).reshape(rows, -1)

time: 125 us -> 125 us (level)
  no operation moved by 1% of the time
where the time goes in v5:
time: 125 us; the launch traced here: 124 us
  blocking collectives  60.6 us (48%)
  starting transfers between devices  33.6 us (27%)
  waiting for transfers between devices  16.3 us (13%)
  Pallas kernels  9.44 us (8%)
  local copies, waits for them, and re-layouts  3.17 us (3%)
    all_to_all x2, blocking collectives, spread(): lax.all_to_all(jnp.broadcast_to(array[None], (size,) + array.shape), axis...  27.7 us
    ppermute x3, starting transfers between devices, shards(): lax.ppermute(outgoing[ahead], 'z_far', [(i, (i + ahead) % planes) for i i...  25.4 us
    all_to_all x1, waiting for transfers between devices, shards(): incoming = lax.all_to_all(picked, NEAR, 0, 0)  14.1 us
    all_to_all x1, blocking collectives, shards(): lax.all_to_all(aggregated, 'feat', 0, 0).reshape(feat * kept, -1)  13.2 us
    all_gather x1, blocking collectives, shards(): weight_all = lax.all_gather(weight, 'feat', axis=0, tiled=True)  10.2 us
    all_to_all x1, blocking collectives, shards(): terms = lax.all_to_all(terms, PLANE, 0, 0).sum(axis=0)  9.55 us
    all_to_all x1, starting transfers between devices, shards(): incoming = lax.all_to_all(picked, NEAR, 0, 0)  8.11 us
    pallas_call x4, Pallas kernels, pick(): pl.pallas_call(pick_kernel, grid=(1,), in_specs=[pl.BlockSpec((rows, bloc...  4.94 us
  transfers between devices with their start and end apart: 4, of which 2 were waited for; matrix products, arithmetic and copies ran while one was open for 0% of the time, Pallas kernels for 3%

profile of v5, /device:TPU:1, one launch (start us, length us, event | category | flops | bytes accessed | tf_op | source)
XLA Modules:
  0.0 124.0 jit_solution(1235680814557987856)
XLA Ops:
  0.6 1.9 %keep_columns.1 = (bf16[288,128]{1,0:T(8,128)(2,1)}, bf16[288,128]{1,0:T(8,128)(2,1)}, bf16[288,128]{1,0:T(8,128)(2,1)}, bf16[288,128]{1,0:T(8,128)(2,1)}) custom-call(s32[1,32]{1,0:T(1,128)} %bitcast.21, bf16[64,1024]{1,0:T(8,128)(2,1)} %bitcast.18, s32[128,128]{1,0:T(8,128)} %bitcast.19), custom_call_target="tpu_custom_call" | custom-call | tf_op jit(solution)/shard_map/keep_columns/pallas_call | solution.py:57
  2.5 16.3 %collective-permute-start.2 = (bf16[288,128]{1,0:T(8,128)(2,1)}, bf16[288,128]{1,0:T(8,128)(2,1)S(1)}, u32[]{:S(2)}, u32[]{:S(2)}) collective-permute-start(bf16[288,128]{1,0:T(8,128)(2,1)} %get-tuple-element.16), channel_id=1, source_target_pairs={{0,256},{128,384},{256,0},{384,128},{1,257},{129,385},{257,1},{385... | collective-permute-start | bytes 221192 | tf_op jit(solution)/shard_map/ppermute | solution.py:249
  18.8 4.0 %collective-permute-start.1 = (bf16[288,128]{1,0:T(8,128)(2,1)}, bf16[288,128]{1,0:T(8,128)(2,1)S(1)}, u32[]{:S(2)}, u32[]{:S(2)}) collective-permute-start(bf16[288,128]{1,0:T(8,128)(2,1)} %get-tuple-element.15), channel_id=1, source_target_pairs={{0,128},{128,256},{256,384},{384,0},{1,129},{129,257},{257,385},{3... | collective-permute-start | bytes 221192 | tf_op jit(solution)/shard_map/ppermute | solution.py:249
  22.8 5.2 %collective-permute-start = (bf16[288,128]{1,0:T(8,128)(2,1)}, bf16[288,128]{1,0:T(8,128)(2,1)S(1)}, u32[]{:S(2)}, u32[]{:S(2)}) collective-permute-start(bf16[288,128]{1,0:T(8,128)(2,1)} %get-tuple-element.14), channel_id=1, source_target_pairs={{0,384},{128,0},{256,128},{384,256},{1,385},{129,1},{257,129},{385... | collective-permute-start | bytes 221192 | tf_op jit(solution)/shard_map/ppermute | solution.py:249
  28.0 0.9 copy-done.1
  28.8 1.2 pick_rows.4.rest_0_
  30.1 1.2 %pick_rows.5.rest_0_ = bf16[32,4,32,128]{3,2,1,0:T(8,128)(2,1)} custom-call(bf16[288,128]{1,0:T(8,128)(2,1)S(1)} %collective-permute-done.2.held_ref, bf16[32,4,32,128]{3,2,1,0:T(8,128)(2,1)} %pick_rows.4.rest_0_), custom_call_target="tpu_custom_call", output_to_operand_aliasing={{}: (1, {})} | custom-call | flops 268435456 | bytes 335872 | tf_op jit(solution)/shard_map/pick_rows/pallas_call | solution.py:103
  31.3 1.3 %pick_rows.6.rest_0_ = bf16[32,4,32,128]{3,2,1,0:T(8,128)(2,1)} custom-call(bf16[288,128]{1,0:T(8,128)(2,1)S(1)} %collective-permute-done.1.held_ref, bf16[32,4,32,128]{3,2,1,0:T(8,128)(2,1)} %pick_rows.5.rest_0_), custom_call_target="tpu_custom_call", output_to_operand_aliasing={{}: (1, {})} | custom-call | flops 268435456 | bytes 335872 | tf_op jit(solution)/shard_map/pick_rows/pallas_call | solution.py:103
  32.6 2.3 %collective-permute-done.held_ref = bf16[288,128]{1,0:T(8,128)(2,1)S(1)} collective-permute-done((bf16[288,128]{1,0:T(8,128)(2,1)}, bf16[288,128]{1,0:T(8,128)(2,1)S(1)}, u32[]{:S(2)}, u32[]{:S(2)}) %collective-permute-start) | collective-permute-done | bytes 73760 | tf_op jit(solution)/shard_map/ppermute | solution.py:249
  34.8 1.2 pick_rows.7
  36.1 8.1 %all-to-all-start = ((bf16[32,128,128]{2,1,0:T(8,128)(2,1)}), bf16[32,128,128]{2,1,0:T(8,128)(2,1)S(1)}, u32[]{:S(2)}, u32[]{:S(2)}) async-start(bf16[32,128,128]{2,1,0:T(8,128)(2,1)} %bitcast.3), calls=%async_computation | async-start | bytes 2097152 | tf_op jit(solution)/shard_map/all_to_all | solution.py:254
  44.2 0.7 copy-done.4
  44.9 10.2 %all_gather.3 = bf16[128,256]{1,0:T(8,128)(2,1)S(1)} all-gather(bf16[32,256]{1,0:T(8,128)(2,1)S(1)} %copy-done.4), channel_id=1, replica_groups=mesh['z_far'=4,'z_near'=4,'y'=4,'core'=2,'feat'=4] {'feat'}, dimensions={0}, use_global_device_ids=true | all-gather | bytes 81920 | tf_op jit(solution)/shard_map/all_gather | solution.py:261
  55.2 0.1 copy.20
  55.3 0.6 copy-done.5
  56.0 0.6 copy-done.6
  56.7 14.1 %all-to-all-done = bf16[32,128,128]{2,1,0:T(8,128)(2,1)S(1)} async-done(((bf16[32,128,128]{2,1,0:T(8,128)(2,1)}), bf16[32,128,128]{2,1,0:T(8,128)(2,1)S(1)}, u32[]{:S(2)}, u32[]{:S(2)}) %all-to-all-start) | async-done | bytes 1048608 | tf_op jit(solution)/shard_map/all_to_all | solution.py:254
  70.8 1.0 aggregate_tiles.1
  71.8 13.2 %all_to_all.25 = f32[4,32,1024]{2,1,0:T(8,128)S(1)} all-to-all(f32[4,32,1024]{2,1,0:T(8,128)S(1)} %aggregate_tiles.1), channel_id=1, replica_groups=mesh['z_far'=4,'z_near'=4,'y'=4,'core'=2,'feat'=4] {'feat'}, dimensions={0} | all-to-all | bytes 1048576 | tf_op jit(solution)/shard_map/all_to_all | solution.py:267
  84.9 1.0 layer_and_gradient.1
  86.0 9.6 %all_to_all.26 = f32[8,16,128]{2,1,0:T(8,128)S(1)} all-to-all(f32[8,16,128]{2,1,0:T(8,128)S(1)} %get-tuple-element.22), channel_id=1, replica_groups=mesh['z_far'=4,'z_near'=4,'y'=4,'core'=2,'feat'=4] {'y','core'}, dimensions={0} | all-to-all | bytes 131072 | tf_op jit(solution)/shard_map/all_to_all | solution.py:270
  95.6 18.3 %all_to_all.27 = f32[16,1,1152]{2,1,0:T(1,128)S(1)} all-to-all(f32[16,1,1152]{2,1,0:T(1,128)S(1)} %broadcast_in_dim.25), channel_id=1, replica_groups=mesh['z_far'=4,'z_near'=4,'y'=4,'core'=2,'feat'=4] {'z_far','z_near'}, dimensions={0} | all-to-all | bytes 147456 | tf_op jit(solution)/shard_map/all_to_all | solution.py:235
  114.0 9.4 %all_to_all.28.terms_ref = f32[8,16,128]{2,1,0:T(8,128)S(1)} all-to-all(f32[8,16,128]{2,1,0:T(8,128)S(1)} %broadcast_in_dim.26), channel_id=1, replica_groups=mesh['z_far'=4,'z_near'=4,'y'=4,'core'=2,'feat'=4] {'y','core'}, dimensions={0} | all-to-all | bytes 131072 | tf_op jit(solution)/shard_map/all_to_all | solution.py:235
  123.4 0.6 unpack_gradients.1
  (24 shorter events, 0.3 us)
Async XLA Ops:
  2.5 27.6 %collective-permute-start.2 = (bf16[288,128]{1,0:T(8,128)(2,1)}, bf16[288,128]{1,0:T(8,128)(2,1)S(1)}, u32[]{:S(2)}, u32[]{:S(2)}) collective-permute-start(bf16[288,128]{1,0:T(8,128)(2,1)} %get-tuple-element.16), channel_id=1, source_target_pairs={{0,256},{128,384},{256,0},{384,128},{1,257},{129,385},{257,1},{385... | collective-permute-start | bytes 221192 | tf_op jit(solution)/shard_map/ppermute | solution.py:249
  18.8 12.6 %collective-permute-start.1 = (bf16[288,128]{1,0:T(8,128)(2,1)}, bf16[288,128]{1,0:T(8,128)(2,1)S(1)}, u32[]{:S(2)}, u32[]{:S(2)}) collective-permute-start(bf16[288,128]{1,0:T(8,128)(2,1)} %get-tuple-element.15), channel_id=1, source_target_pairs={{0,128},{128,256},{256,384},{384,0},{1,129},{129,257},{257,385},{3... | collective-permute-start | bytes 221192 | tf_op jit(solution)/shard_map/ppermute | solution.py:249
  22.8 12.1 %collective-permute-start = (bf16[288,128]{1,0:T(8,128)(2,1)}, bf16[288,128]{1,0:T(8,128)(2,1)S(1)}, u32[]{:S(2)}, u32[]{:S(2)}) collective-permute-start(bf16[288,128]{1,0:T(8,128)(2,1)} %get-tuple-element.14), channel_id=1, source_target_pairs={{0,384},{128,0},{256,128},{384,256},{1,385},{129,1},{257,129},{385... | collective-permute-start | bytes 221192 | tf_op jit(solution)/shard_map/ppermute | solution.py:249
  28.0 0.9 copy-start.1
  36.0 8.1 %copy-start.2 = (bf16[288,128]{1,0:T(8,128)(2,1)S(1)}, bf16[288,128]{1,0:T(8,128)(2,1)}, u32[]{:S(2)}) copy-start(bf16[288,128]{1,0:T(8,128)(2,1)} %get-tuple-element.17.held_ref) | copy-start | bytes 221188
  36.1 34.7 %copy-start = (bf16[32,128,128]{2,1,0:T(8,128)(2,1)S(1)}, bf16[32,128,128]{2,1,0:T(8,128)(2,1)}, u32[]{:S(2)}) copy-start(bf16[32,128,128]{2,1,0:T(8,128)(2,1)} %vals_ref.1) | copy-start | bytes 3145732
  36.1 34.7 %all-to-all-start = ((bf16[32,128,128]{2,1,0:T(8,128)(2,1)}), bf16[32,128,128]{2,1,0:T(8,128)(2,1)S(1)}, u32[]{:S(2)}, u32[]{:S(2)}) async-start(bf16[32,128,128]{2,1,0:T(8,128)(2,1)} %bitcast.3), calls=%async_computation | async-start | bytes 2097152 | tf_op jit(solution)/shard_map/all_to_all | solution.py:254
  44.2 0.7 copy-start.4
  55.3 0.7 copy-start.5
  56.0 0.7 copy-start.6
  71.8 13.2 %copy-start.3 = (bf16[1024,64]{0,1:T(8,128)(2,1)S(1)}, bf16[1024,64]{0,1:T(8,128)(2,1)}, u32[]{:S(2)}) copy-start(bf16[1024,64]{0,1:T(8,128)(2,1)} %param.15) | copy-start | bytes 393220

commit v6 on v5

--- a/solution.py
+++ b/solution.py
@@ -44,7 +44,7 @@
     for ahead, out_ref in enumerate(out_refs):
         for tile in range(nodes // block):
             out_ref[tile * kept : (tile + 1) * kept, :] = columns[:, tile * block : (tile + 1) * block]
-        first = pl.multiple_of(lax.rem(me + ahead, planes) * lists, lists)
+        first = pl.multiple_of(lax.bitwise_xor(me, ahead) * lists, lists)
         out_ref[rows - lists :, :] = code_ref[pl.ds(first, lists), :]
 
 
@@ -246,7 +246,7 @@
     own = outgoing[0][: features.shape[0] // block * kept]
     held = [outgoing[0]] + [None] * (planes - 1)
     for ahead in ORDER:
-        held[ahead] = lax.ppermute(outgoing[ahead], "z_far", [(i, (i + ahead) % planes) for i in range(planes)])
+        held[ahead] = lax.ppermute(outgoing[ahead], "z_far", [(i, i ^ ahead) for i in range(planes)])
     picked = None
     for ahead in (0,) + ORDER:
         picked = pick(held[ahead], ahead, planes, near, kept, picked)
@@ -255,7 +255,7 @@
     incoming = incoming.reshape(near * planes, kept, block)
     tiles = features.shape[0] // block
     sender = tile_cols - tiles
-    behind = lax.rem(lax.axis_index("z_far") + planes - lax.div(sender, near), planes)
+    behind = lax.bitwise_xor(lax.axis_index("z_far"), lax.div(sender, near))
     place = tiles + lax.rem(sender, near) * planes + behind
     tile_cols = jnp.where(sender < 0, tile_cols, place)
     weight_all = lax.all_gather(weight, "feat", axis=0, tiled=True)

time: 125 us -> 125 us (level)
  waiting for transfers between devices: 16.3 us -> 21.2 us
  starting transfers between devices: 33.6 us -> 29.8 us
    ppermute x3, waiting for transfers between devices: 2.26 us -> 7.13 us  [shards(): lax.ppermute(outgoing[ahead], 'z_far', [(i, i ^ ahead) for i in range(pla...]
    ppermute x3, starting transfers between devices: 25.4 us -> 22.2 us  [shards(): lax.ppermute(outgoing[ahead], 'z_far', [(i, i ^ ahead) for i in range(pla...]
  transfers between devices with their start and end apart: 4 -> 4, of which waited for: 2 -> 3; matrix products, arithmetic and copies ran while one was open for 0% -> 0% of each run, Pallas kernels for 3% -> 3%
where the time goes in v6:
time: 125 us; the launch traced here: 124 us
  blocking collectives  59.5 us (48%)
  starting transfers between devices  29.8 us (24%)
  waiting for transfers between devices  21.2 us (17%)
  Pallas kernels  9.43 us (8%)
  local copies, waits for them, and re-layouts  3.17 us (3%)
    all_to_all x2, blocking collectives, spread(): lax.all_to_all(jnp.broadcast_to(array[None], (size,) + array.shape), axis...  26.6 us
    ppermute x3, starting transfers between devices, shards(): lax.ppermute(outgoing[ahead], 'z_far', [(i, i ^ ahead) for i in range(pla...  22.2 us
    all_to_all x1, waiting for transfers between devices, shards(): incoming = lax.all_to_all(picked, NEAR, 0, 0)  14.1 us
    all_to_all x1, blocking collectives, shards(): lax.all_to_all(aggregated, 'feat', 0, 0).reshape(feat * kept, -1)  13.2 us
    all_gather x1, blocking collectives, shards(): weight_all = lax.all_gather(weight, 'feat', axis=0, tiled=True)  10.2 us
    all_to_all x1, blocking collectives, shards(): terms = lax.all_to_all(terms, PLANE, 0, 0).sum(axis=0)  9.55 us
    all_to_all x1, starting transfers between devices, shards(): incoming = lax.all_to_all(picked, NEAR, 0, 0)  7.63 us
    ppermute x3, waiting for transfers between devices, shards(): lax.ppermute(outgoing[ahead], 'z_far', [(i, i ^ ahead) for i in range(pla...  7.13 us
  transfers between devices with their start and end apart: 4, of which 3 were waited for; matrix products, arithmetic and copies ran while one was open for 0% of the time, Pallas kernels for 3%

profile of v6, /device:TPU:1, one launch (start us, length us, event | category | flops | bytes accessed | tf_op | source)
XLA Modules:
  0.0 124.0 jit_solution(343783771092153355)
XLA Ops:
  0.6 1.9 %keep_columns.1 = (bf16[288,128]{1,0:T(8,128)(2,1)}, bf16[288,128]{1,0:T(8,128)(2,1)}, bf16[288,128]{1,0:T(8,128)(2,1)}, bf16[288,128]{1,0:T(8,128)(2,1)}) custom-call(s32[1,32]{1,0:T(1,128)} %bitcast.21, bf16[64,1024]{1,0:T(8,128)(2,1)} %bitcast.18, s32[128,128]{1,0:T(8,128)} %bitcast.19), custom_call_target="tpu_custom_call" | custom-call | tf_op jit(solution)/shard_map/keep_columns/pallas_call | solution.py:57
  2.5 16.3 %collective-permute-start.2 = (bf16[288,128]{1,0:T(8,128)(2,1)}, bf16[288,128]{1,0:T(8,128)(2,1)S(1)}, u32[]{:S(2)}, u32[]{:S(2)}) collective-permute-start(bf16[288,128]{1,0:T(8,128)(2,1)} %get-tuple-element.16), channel_id=1, source_target_pairs={{0,256},{128,384},{256,0},{384,128},{1,257},{129,385},{257,1},{385... | collective-permute-start | bytes 221192 | tf_op jit(solution)/shard_map/ppermute | solution.py:249
  18.8 4.0 %collective-permute-start.1 = (bf16[288,128]{1,0:T(8,128)(2,1)}, bf16[288,128]{1,0:T(8,128)(2,1)S(1)}, u32[]{:S(2)}, u32[]{:S(2)}) collective-permute-start(bf16[288,128]{1,0:T(8,128)(2,1)} %get-tuple-element.15), channel_id=1, source_target_pairs={{0,128},{128,0},{256,384},{384,256},{1,129},{129,1},{257,385},{385... | collective-permute-start | bytes 221192 | tf_op jit(solution)/shard_map/ppermute | solution.py:249
  22.8 1.9 %collective-permute-start = (bf16[288,128]{1,0:T(8,128)(2,1)}, bf16[288,128]{1,0:T(8,128)(2,1)S(1)}, u32[]{:S(2)}, u32[]{:S(2)}) collective-permute-start(bf16[288,128]{1,0:T(8,128)(2,1)} %get-tuple-element.14), channel_id=1, source_target_pairs={{0,384},{128,256},{256,128},{384,0},{1,385},{129,257},{257,129},{3... | collective-permute-start | bytes 221192 | tf_op jit(solution)/shard_map/ppermute | solution.py:249
  24.7 0.9 copy-done.1
  25.6 1.2 pick_rows.4.rest_0_
  26.8 1.2 %pick_rows.5.rest_0_ = bf16[32,4,32,128]{3,2,1,0:T(8,128)(2,1)} custom-call(bf16[288,128]{1,0:T(8,128)(2,1)S(1)} %collective-permute-done.2.held_ref, bf16[32,4,32,128]{3,2,1,0:T(8,128)(2,1)} %pick_rows.4.rest_0_), custom_call_target="tpu_custom_call", output_to_operand_aliasing={{}: (1, {})} | custom-call | flops 268435456 | bytes 335872 | tf_op jit(solution)/shard_map/pick_rows/pallas_call | solution.py:103
  28.1 5.1 %collective-permute-done.1.held_ref = bf16[288,128]{1,0:T(8,128)(2,1)S(1)} collective-permute-done((bf16[288,128]{1,0:T(8,128)(2,1)}, bf16[288,128]{1,0:T(8,128)(2,1)S(1)}, u32[]{:S(2)}, u32[]{:S(2)}) %collective-permute-start.1) | collective-permute-done | bytes 73760 | tf_op jit(solution)/shard_map/ppermute | solution.py:249
  33.2 1.3 %pick_rows.6.rest_0_ = bf16[32,4,32,128]{3,2,1,0:T(8,128)(2,1)} custom-call(bf16[288,128]{1,0:T(8,128)(2,1)S(1)} %collective-permute-done.1.held_ref, bf16[32,4,32,128]{3,2,1,0:T(8,128)(2,1)} %pick_rows.5.rest_0_), custom_call_target="tpu_custom_call", output_to_operand_aliasing={{}: (1, {})} | custom-call | flops 268435456 | bytes 335872 | tf_op jit(solution)/shard_map/pick_rows/pallas_call | solution.py:103
  34.4 2.0 %collective-permute-done.held_ref = bf16[288,128]{1,0:T(8,128)(2,1)S(1)} collective-permute-done((bf16[288,128]{1,0:T(8,128)(2,1)}, bf16[288,128]{1,0:T(8,128)(2,1)S(1)}, u32[]{:S(2)}, u32[]{:S(2)}) %collective-permute-start) | collective-permute-done | bytes 73760 | tf_op jit(solution)/shard_map/ppermute | solution.py:249
  36.5 1.2 pick_rows.7
  37.7 7.6 %all-to-all-start = ((bf16[32,128,128]{2,1,0:T(8,128)(2,1)}), bf16[32,128,128]{2,1,0:T(8,128)(2,1)S(1)}, u32[]{:S(2)}, u32[]{:S(2)}) async-start(bf16[32,128,128]{2,1,0:T(8,128)(2,1)} %bitcast.3), calls=%async_computation | async-start | bytes 2097152 | tf_op jit(solution)/shard_map/all_to_all | solution.py:254
  45.3 0.7 copy-done.4
  46.0 10.2 %all_gather.3 = bf16[128,256]{1,0:T(8,128)(2,1)S(1)} all-gather(bf16[32,256]{1,0:T(8,128)(2,1)S(1)} %copy-done.4), channel_id=1, replica_groups=mesh['z_far'=4,'z_near'=4,'y'=4,'core'=2,'feat'=4] {'feat'}, dimensions={0}, use_global_device_ids=true | all-gather | bytes 81920 | tf_op jit(solution)/shard_map/all_gather | solution.py:261
  56.4 0.6 copy-done.5
  57.1 0.6 copy-done.6
  57.8 14.1 %all-to-all-done = bf16[32,128,128]{2,1,0:T(8,128)(2,1)S(1)} async-done(((bf16[32,128,128]{2,1,0:T(8,128)(2,1)}), bf16[32,128,128]{2,1,0:T(8,128)(2,1)S(1)}, u32[]{:S(2)}, u32[]{:S(2)}) %all-to-all-start) | async-done | bytes 1048608 | tf_op jit(solution)/shard_map/all_to_all | solution.py:254
  71.9 1.0 aggregate_tiles.1
  72.9 13.2 %all_to_all.25 = f32[4,32,1024]{2,1,0:T(8,128)S(1)} all-to-all(f32[4,32,1024]{2,1,0:T(8,128)S(1)} %aggregate_tiles.1), channel_id=1, replica_groups=mesh['z_far'=4,'z_near'=4,'y'=4,'core'=2,'feat'=4] {'feat'}, dimensions={0} | all-to-all | bytes 1048576 | tf_op jit(solution)/shard_map/all_to_all | solution.py:267
  86.1 1.0 layer_and_gradient.1
  87.1 9.6 %all_to_all.26 = f32[8,16,128]{2,1,0:T(8,128)S(1)} all-to-all(f32[8,16,128]{2,1,0:T(8,128)S(1)} %get-tuple-element.22), channel_id=1, replica_groups=mesh['z_far'=4,'z_near'=4,'y'=4,'core'=2,'feat'=4] {'y','core'}, dimensions={0} | all-to-all | bytes 131072 | tf_op jit(solution)/shard_map/all_to_all | solution.py:270
  96.7 17.2 %all_to_all.27 = f32[16,1,1152]{2,1,0:T(1,128)S(1)} all-to-all(f32[16,1,1152]{2,1,0:T(1,128)S(1)} %broadcast_in_dim.25), channel_id=1, replica_groups=mesh['z_far'=4,'z_near'=4,'y'=4,'core'=2,'feat'=4] {'z_far','z_near'}, dimensions={0} | all-to-all | bytes 147456 | tf_op jit(solution)/shard_map/all_to_all | solution.py:235
  114.0 9.4 %all_to_all.28.terms_ref = f32[8,16,128]{2,1,0:T(8,128)S(1)} all-to-all(f32[8,16,128]{2,1,0:T(8,128)S(1)} %broadcast_in_dim.26), channel_id=1, replica_groups=mesh['z_far'=4,'z_near'=4,'y'=4,'core'=2,'feat'=4] {'y','core'}, dimensions={0} | all-to-all | bytes 131072 | tf_op jit(solution)/shard_map/all_to_all | solution.py:235
  123.4 0.6 unpack_gradients.1
  (24 shorter events, 0.4 us)
Async XLA Ops:
  2.5 24.3 %collective-permute-start.2 = (bf16[288,128]{1,0:T(8,128)(2,1)}, bf16[288,128]{1,0:T(8,128)(2,1)S(1)}, u32[]{:S(2)}, u32[]{:S(2)}) collective-permute-start(bf16[288,128]{1,0:T(8,128)(2,1)} %get-tuple-element.16), channel_id=1, source_target_pairs={{0,256},{128,384},{256,0},{384,128},{1,257},{129,385},{257,1},{385... | collective-permute-start | bytes 221192 | tf_op jit(solution)/shard_map/ppermute | solution.py:249
  18.8 14.4 %collective-permute-start.1 = (bf16[288,128]{1,0:T(8,128)(2,1)}, bf16[288,128]{1,0:T(8,128)(2,1)S(1)}, u32[]{:S(2)}, u32[]{:S(2)}) collective-permute-start(bf16[288,128]{1,0:T(8,128)(2,1)} %get-tuple-element.15), channel_id=1, source_target_pairs={{0,128},{128,0},{256,384},{384,256},{1,129},{129,1},{257,385},{385... | collective-permute-start | bytes 221192 | tf_op jit(solution)/shard_map/ppermute | solution.py:249
  22.8 13.7 %collective-permute-start = (bf16[288,128]{1,0:T(8,128)(2,1)}, bf16[288,128]{1,0:T(8,128)(2,1)S(1)}, u32[]{:S(2)}, u32[]{:S(2)}) collective-permute-start(bf16[288,128]{1,0:T(8,128)(2,1)} %get-tuple-element.14), channel_id=1, source_target_pairs={{0,384},{128,256},{256,128},{384,0},{1,385},{129,257},{257,129},{3... | collective-permute-start | bytes 221192 | tf_op jit(solution)/shard_map/ppermute | solution.py:249
  24.7 0.9 copy-start.1
  37.7 7.6 %copy-start.2 = (bf16[288,128]{1,0:T(8,128)(2,1)S(1)}, bf16[288,128]{1,0:T(8,128)(2,1)}, u32[]{:S(2)}) copy-start(bf16[288,128]{1,0:T(8,128)(2,1)} %get-tuple-element.17.held_ref) | copy-start | bytes 221188
  37.7 34.2 %copy-start = (bf16[32,128,128]{2,1,0:T(8,128)(2,1)S(1)}, bf16[32,128,128]{2,1,0:T(8,128)(2,1)}, u32[]{:S(2)}) copy-start(bf16[32,128,128]{2,1,0:T(8,128)(2,1)} %vals_ref.1) | copy-start | bytes 3145732
  37.7 34.2 %all-to-all-start = ((bf16[32,128,128]{2,1,0:T(8,128)(2,1)}), bf16[32,128,128]{2,1,0:T(8,128)(2,1)S(1)}, u32[]{:S(2)}, u32[]{:S(2)}) async-start(bf16[32,128,128]{2,1,0:T(8,128)(2,1)} %bitcast.3), calls=%async_computation | async-start | bytes 2097152 | tf_op jit(solution)/shard_map/all_to_all | solution.py:254
  45.3 0.7 copy-start.4
  56.4 0.7 copy-start.5
  57.1 0.7 copy-start.6
  72.9 13.2 %copy-start.3 = (bf16[1024,64]{0,1:T(8,128)(2,1)S(1)}, bf16[1024,64]{0,1:T(8,128)(2,1)}, u32[]{:S(2)}) copy-start(bf16[1024,64]{0,1:T(8,128)(2,1)} %param.15) | copy-start | bytes 393220

commit v7 on v5

--- a/solution.py
+++ b/solution.py
@@ -26,40 +26,65 @@
     return jnp.sum(jnp.where(same, row, 0.0), axis=1, keepdims=True)
 
 
-def keep_kernel(keep_ref, features_ref, lists_ref, *refs):
-    out_refs, code_ref = refs[:-1], refs[-1]
-    planes = len(out_refs)
-    rows, block = out_refs[0].shape
+def keep_kernel(planes, *refs):
+    sources, out_refs = refs[:3], refs[3 : 3 + planes]
+    keep_ref, features_ref, lists_ref, kept_ref, code_ref, read_sems, write_sems = refs[3 + planes :]
+    reads = [
+        pltpu.make_async_copy(source, target, read_sems.at[place])
+        for place, (source, target) in enumerate(zip(sources, (keep_ref, features_ref, lists_ref)))
+    ]
+    for read in reads[::-1]:
+        read.start()
     kept = keep_ref.shape[1]
+    block = lists_ref.shape[1]
     nodes = features_ref.shape[1]
     lists = lists_ref.shape[0] // planes
-    lane = lax.broadcasted_iota(jnp.int32, (kept, features_ref.shape[0]), 1)
-    wanted = as_column(keep_ref[...].astype(F32)).astype(jnp.int32)
-    select = jnp.where(lane == wanted, 1.0, 0.0).astype(BF16)
-    columns = jnp.dot(select, features_ref[...], preferred_element_type=F32).astype(BF16)
+    rows = kept_ref.shape[0]
+    writes = []
+    reads[2].wait()
     row = lists_ref[...]
     code = lax.shift_left(CODE + (row & (CODE - 1)), row // CODE)
     code_ref[...] = (code.astype(F32) * (1.0 / CODE)).astype(BF16)
     me = lax.axis_index("z_far")
     for ahead, out_ref in enumerate(out_refs):
-        for tile in range(nodes // block):
-            out_ref[tile * kept : (tile + 1) * kept, :] = columns[:, tile * block : (tile + 1) * block]
         first = pl.multiple_of(lax.rem(me + ahead, planes) * lists, lists)
-        out_ref[rows - lists :, :] = code_ref[pl.ds(first, lists), :]
+        source = code_ref.at[pl.ds(first, lists), :]
+        writes.append(pltpu.make_async_copy(source, out_ref.at[pl.ds(rows, lists), :], write_sems.at[2 * ahead]))
+        writes[-1].start()
+    reads[0].wait()
+    lane = lax.broadcasted_iota(jnp.int32, (kept, features_ref.shape[0]), 1)
+    wanted = as_column(keep_ref[...].astype(F32)).astype(jnp.int32)
+    select = jnp.where(lane == wanted, 1.0, 0.0).astype(BF16)
+    reads[1].wait()
+    columns = jnp.dot(select, features_ref[...], preferred_element_type=F32).astype(BF16)
+    for tile in range(nodes // block):
+        kept_ref[tile * kept : (tile + 1) * kept, :] = columns[:, tile * block : (tile + 1) * block]
+    for ahead, out_ref in enumerate(out_refs):
+        writes.append(pltpu.make_async_copy(kept_ref, out_ref.at[pl.ds(0, rows), :], write_sems.at[2 * ahead + 1]))
+        writes[-1].start()
+    for write in writes:
+        write.wait()
 
 
 def keep(keep_cols, features, lists, planes):
     peers, block = lists.shape
-    nodes = features.shape[1]
     kept = keep_cols.shape[0]
-    rows = nodes // block * kept + peers // planes
-    vmem = pl.BlockSpec(memory_space=pltpu.VMEM)
-    return pl.pallas_call(
-        keep_kernel,
-        in_specs=[vmem] * 3,
-        out_specs=[vmem] * planes,
-        out_shape=[jax.ShapeDtypeStruct((rows, block), BF16)] * planes,
-        scratch_shapes=[pltpu.VMEM(lists.shape, BF16)],
+    rows = features.shape[1] // block * kept
+    hbm = pl.BlockSpec(memory_space=pl.ANY)
+    return pl.pallas_call(
+        functools.partial(keep_kernel, planes),
+        in_specs=[hbm] * 3,
+        out_specs=[hbm] * planes,
+        out_shape=[jax.ShapeDtypeStruct((rows + peers // planes, block), BF16)] * planes,
+        scratch_shapes=[
+            pltpu.VMEM((1, kept), jnp.int32),
+            pltpu.VMEM(features.shape, BF16),
+            pltpu.VMEM(lists.shape, jnp.int32),
+            pltpu.VMEM((rows, block), BF16),
+            pltpu.VMEM(lists.shape, BF16),
+            pltpu.SemaphoreType.DMA((3,)),
+            pltpu.SemaphoreType.DMA((2 * planes,)),
+        ],
         name="keep_columns",
     )(keep_cols[None, :], features, lists)
 

time: 125 us -> 125 us (level)
  no operation moved by 1% of the time
where the time goes in v7:
time: 125 us; the launch traced here: 124 us
  blocking collectives  60.7 us (49%)
  starting transfers between devices  33.5 us (27%)
  waiting for transfers between devices  16.3 us (13%)
  Pallas kernels  9.47 us (8%)
  local copies, waits for them, and re-layouts  3.17 us (3%)
    all_to_all x2, blocking collectives, spread(): lax.all_to_all(jnp.broadcast_to(array[None], (size,) + array.shape), axis...  27.6 us
    ppermute x3, starting transfers between devices, shards(): lax.ppermute(outgoing[ahead], 'z_far', [(i, (i + ahead) % planes) for i i...  25.5 us
    all_to_all x1, waiting for transfers between devices, shards(): incoming = lax.all_to_all(picked, NEAR, 0, 0)  14 us
    all_to_all x1, blocking collectives, shards(): lax.all_to_all(aggregated, 'feat', 0, 0).reshape(feat * kept, -1)  13.3 us
    all_gather x1, blocking collectives, shards(): weight_all = lax.all_gather(weight, 'feat', axis=0, tiled=True)  10.3 us
    all_to_all x1, blocking collectives, shards(): terms = lax.all_to_all(terms, PLANE, 0, 0).sum(axis=0)  9.55 us
    all_to_all x1, starting transfers between devices, shards(): incoming = lax.all_to_all(picked, NEAR, 0, 0)  8.02 us
    pallas_call x4, Pallas kernels, pick(): pl.pallas_call(pick_kernel, grid=(1,), in_specs=[pl.BlockSpec((rows, bloc...  4.92 us
  transfers between devices with their start and end apart: 4, of which 2 were waited for; matrix products, arithmetic and copies ran while one was open for 0% of the time, Pallas kernels for 3%

profile of v7, /device:TPU:1, one launch (start us, length us, event | category | flops | bytes accessed | tf_op | source)
XLA Modules:
  0.0 124.1 jit_solution(5463684345270534247)
XLA Ops:
  0.6 1.9 %keep_columns.1 = (bf16[288,128]{1,0:T(8,128)(2,1)}, bf16[288,128]{1,0:T(8,128)(2,1)}, bf16[288,128]{1,0:T(8,128)(2,1)}, bf16[288,128]{1,0:T(8,128)(2,1)}) custom-call(s32[1,32]{1,0:T(1,128)} %bitcast.21, bf16[64,1024]{1,0:T(8,128)(2,1)} %bitcast.18, s32[128,128]{1,0:T(8,128)} %bitcast.19), custom_call_target="tpu_custom_call" | custom-call | tf_op jit(solution)/shard_map/keep_columns/pallas_call | solution.py:74
  2.5 16.3 %collective-permute-start.2 = (bf16[288,128]{1,0:T(8,128)(2,1)}, bf16[288,128]{1,0:T(8,128)(2,1)S(1)}, u32[]{:S(2)}, u32[]{:S(2)}) collective-permute-start(bf16[288,128]{1,0:T(8,128)(2,1)} %get-tuple-element.16), channel_id=1, source_target_pairs={{0,256},{128,384},{256,0},{384,128},{1,257},{129,385},{257,1},{385... | collective-permute-start | bytes 221192 | tf_op jit(solution)/shard_map/ppermute | solution.py:274
  18.8 4.0 %collective-permute-start.1 = (bf16[288,128]{1,0:T(8,128)(2,1)}, bf16[288,128]{1,0:T(8,128)(2,1)S(1)}, u32[]{:S(2)}, u32[]{:S(2)}) collective-permute-start(bf16[288,128]{1,0:T(8,128)(2,1)} %get-tuple-element.15), channel_id=1, source_target_pairs={{0,128},{128,256},{256,384},{384,0},{1,129},{129,257},{257,385},{3... | collective-permute-start | bytes 221192 | tf_op jit(solution)/shard_map/ppermute | solution.py:274
  22.8 5.2 %collective-permute-start = (bf16[288,128]{1,0:T(8,128)(2,1)}, bf16[288,128]{1,0:T(8,128)(2,1)S(1)}, u32[]{:S(2)}, u32[]{:S(2)}) collective-permute-start(bf16[288,128]{1,0:T(8,128)(2,1)} %get-tuple-element.14), channel_id=1, source_target_pairs={{0,384},{128,0},{256,128},{384,256},{1,385},{129,1},{257,129},{385... | collective-permute-start | bytes 221192 | tf_op jit(solution)/shard_map/ppermute | solution.py:274
  28.0 0.9 copy-done.1
  28.9 1.2 pick_rows.4.rest_0_
  30.1 1.2 %pick_rows.5.rest_0_ = bf16[32,4,32,128]{3,2,1,0:T(8,128)(2,1)} custom-call(bf16[288,128]{1,0:T(8,128)(2,1)S(1)} %collective-permute-done.2.held_ref, bf16[32,4,32,128]{3,2,1,0:T(8,128)(2,1)} %pick_rows.4.rest_0_), custom_call_target="tpu_custom_call", output_to_operand_aliasing={{}: (1, {})} | custom-call | flops 268435456 | bytes 335872 | tf_op jit(solution)/shard_map/pick_rows/pallas_call | solution.py:128
  31.4 1.3 %pick_rows.6.rest_0_ = bf16[32,4,32,128]{3,2,1,0:T(8,128)(2,1)} custom-call(bf16[288,128]{1,0:T(8,128)(2,1)S(1)} %collective-permute-done.1.held_ref, bf16[32,4,32,128]{3,2,1,0:T(8,128)(2,1)} %pick_rows.5.rest_0_), custom_call_target="tpu_custom_call", output_to_operand_aliasing={{}: (1, {})} | custom-call | flops 268435456 | bytes 335872 | tf_op jit(solution)/shard_map/pick_rows/pallas_call | solution.py:128
  32.6 2.4 %collective-permute-done.held_ref = bf16[288,128]{1,0:T(8,128)(2,1)S(1)} collective-permute-done((bf16[288,128]{1,0:T(8,128)(2,1)}, bf16[288,128]{1,0:T(8,128)(2,1)S(1)}, u32[]{:S(2)}, u32[]{:S(2)}) %collective-permute-start) | collective-permute-done | bytes 73760 | tf_op jit(solution)/shard_map/ppermute | solution.py:274
  35.0 1.2 pick_rows.7
  36.2 8.0 %all-to-all-start = ((bf16[32,128,128]{2,1,0:T(8,128)(2,1)}), bf16[32,128,128]{2,1,0:T(8,128)(2,1)S(1)}, u32[]{:S(2)}, u32[]{:S(2)}) async-start(bf16[32,128,128]{2,1,0:T(8,128)(2,1)} %bitcast.3), calls=%async_computation | async-start | bytes 2097152 | tf_op jit(solution)/shard_map/all_to_all | solution.py:279
  44.3 0.7 copy-done.4
  45.0 10.3 %all_gather.3 = bf16[128,256]{1,0:T(8,128)(2,1)S(1)} all-gather(bf16[32,256]{1,0:T(8,128)(2,1)S(1)} %copy-done.4), channel_id=1, replica_groups=mesh['z_far'=4,'z_near'=4,'y'=4,'core'=2,'feat'=4] {'feat'}, dimensions={0}, use_global_device_ids=true | all-gather | bytes 81920 | tf_op jit(solution)/shard_map/all_gather | solution.py:286
  55.4 0.1 copy.20
  55.5 0.6 copy-done.5
  56.2 0.6 copy-done.6
  56.9 14.0 %all-to-all-done = bf16[32,128,128]{2,1,0:T(8,128)(2,1)S(1)} async-done(((bf16[32,128,128]{2,1,0:T(8,128)(2,1)}), bf16[32,128,128]{2,1,0:T(8,128)(2,1)S(1)}, u32[]{:S(2)}, u32[]{:S(2)}) %all-to-all-start) | async-done | bytes 1048608 | tf_op jit(solution)/shard_map/all_to_all | solution.py:279
  70.8 1.0 aggregate_tiles.1
  71.8 13.3 %all_to_all.25 = f32[4,32,1024]{2,1,0:T(8,128)S(1)} all-to-all(f32[4,32,1024]{2,1,0:T(8,128)S(1)} %aggregate_tiles.1), channel_id=1, replica_groups=mesh['z_far'=4,'z_near'=4,'y'=4,'core'=2,'feat'=4] {'feat'}, dimensions={0} | all-to-all | bytes 1048576 | tf_op jit(solution)/shard_map/all_to_all | solution.py:292
  85.1 1.0 layer_and_gradient.1
  86.2 9.6 %all_to_all.26 = f32[8,16,128]{2,1,0:T(8,128)S(1)} all-to-all(f32[8,16,128]{2,1,0:T(8,128)S(1)} %get-tuple-element.22), channel_id=1, replica_groups=mesh['z_far'=4,'z_near'=4,'y'=4,'core'=2,'feat'=4] {'y','core'}, dimensions={0} | all-to-all | bytes 131072 | tf_op jit(solution)/shard_map/all_to_all | solution.py:295
  95.8 18.2 %all_to_all.27 = f32[16,1,1152]{2,1,0:T(1,128)S(1)} all-to-all(f32[16,1,1152]{2,1,0:T(1,128)S(1)} %broadcast_in_dim.25), channel_id=1, replica_groups=mesh['z_far'=4,'z_near'=4,'y'=4,'core'=2,'feat'=4] {'z_far','z_near'}, dimensions={0} | all-to-all | bytes 147456 | tf_op jit(solution)/shard_map/all_to_all | solution.py:260
  114.0 9.4 %all_to_all.28.terms_ref = f32[8,16,128]{2,1,0:T(8,128)S(1)} all-to-all(f32[8,16,128]{2,1,0:T(8,128)S(1)} %broadcast_in_dim.26), channel_id=1, replica_groups=mesh['z_far'=4,'z_near'=4,'y'=4,'core'=2,'feat'=4] {'y','core'}, dimensions={0} | all-to-all | bytes 131072 | tf_op jit(solution)/shard_map/all_to_all | solution.py:260
  123.5 0.6 unpack_gradients.1
  (24 shorter events, 0.3 us)
Async XLA Ops:
  2.5 27.6 %collective-permute-start.2 = (bf16[288,128]{1,0:T(8,128)(2,1)}, bf16[288,128]{1,0:T(8,128)(2,1)S(1)}, u32[]{:S(2)}, u32[]{:S(2)}) collective-permute-start(bf16[288,128]{1,0:T(8,128)(2,1)} %get-tuple-element.16), channel_id=1, source_target_pairs={{0,256},{128,384},{256,0},{384,128},{1,257},{129,385},{257,1},{385... | collective-permute-start | bytes 221192 | tf_op jit(solution)/shard_map/ppermute | solution.py:274
  18.8 12.6 %collective-permute-start.1 = (bf16[288,128]{1,0:T(8,128)(2,1)}, bf16[288,128]{1,0:T(8,128)(2,1)S(1)}, u32[]{:S(2)}, u32[]{:S(2)}) collective-permute-start(bf16[288,128]{1,0:T(8,128)(2,1)} %get-tuple-element.15), channel_id=1, source_target_pairs={{0,128},{128,256},{256,384},{384,0},{1,129},{129,257},{257,385},{3... | collective-permute-start | bytes 221192 | tf_op jit(solution)/shard_map/ppermute | solution.py:274
  22.8 12.2 %collective-permute-start = (bf16[288,128]{1,0:T(8,128)(2,1)}, bf16[288,128]{1,0:T(8,128)(2,1)S(1)}, u32[]{:S(2)}, u32[]{:S(2)}) collective-permute-start(bf16[288,128]{1,0:T(8,128)(2,1)} %get-tuple-element.14), channel_id=1, source_target_pairs={{0,384},{128,0},{256,128},{384,256},{1,385},{129,1},{257,129},{385... | collective-permute-start | bytes 221192 | tf_op jit(solution)/shard_map/ppermute | solution.py:274
  28.0 0.9 copy-start.1
  36.2 8.0 %copy-start.2 = (bf16[288,128]{1,0:T(8,128)(2,1)S(1)}, bf16[288,128]{1,0:T(8,128)(2,1)}, u32[]{:S(2)}) copy-start(bf16[288,128]{1,0:T(8,128)(2,1)} %get-tuple-element.17.held_ref) | copy-start | bytes 221188
  36.2 34.6 %copy-start = (bf16[32,128,128]{2,1,0:T(8,128)(2,1)S(1)}, bf16[32,128,128]{2,1,0:T(8,128)(2,1)}, u32[]{:S(2)}) copy-start(bf16[32,128,128]{2,1,0:T(8,128)(2,1)} %vals_ref.1) | copy-start | bytes 3145732
  36.2 34.6 %all-to-all-start = ((bf16[32,128,128]{2,1,0:T(8,128)(2,1)}), bf16[32,128,128]{2,1,0:T(8,128)(2,1)S(1)}, u32[]{:S(2)}, u32[]{:S(2)}) async-start(bf16[32,128,128]{2,1,0:T(8,128)(2,1)} %bitcast.3), calls=%async_computation | async-start | bytes 2097152 | tf_op jit(solution)/shard_map/all_to_all | solution.py:279
  44.3 0.7 copy-start.4
  55.4 0.7 copy-start.5
  56.2 0.7 copy-start.6
  71.8 13.3 %copy-start.3 = (bf16[1024,64]{0,1:T(8,128)(2,1)S(1)}, bf16[1024,64]{0,1:T(8,128)(2,1)}, u32[]{:S(2)}) copy-start(bf16[1024,64]{0,1:T(8,128)(2,1)} %param.15) | copy-start | bytes 393220
